TPU v7x, 32 devices: a whole 2x2x4 slice. The times are simulated.
32 devices in a mesh: gx: 4 (over y, core), gy: 8 (over z, x).
Axes of the slice: x: 2, y: 2, z: 4, core: 2. Of those that a mesh axis runs over, the one named last changes fastest.
Arguments:
- site_tensors: bfloat16 [32, 16, 256, 256], P('gx', 'gy'), may hold values from -6 to 6
- test_matrix: bfloat16 [32, 16, 16, 256], P('gx', 'gy'), may hold values from -0.375 to 0.375
Outputs:
- coarse: bfloat16 [16, 16, 256, 256], P('gx', 'gy')
- log_norm: float32 [16, 16], P('gx', 'gy')
- trace: float32 [16, 16], P('gx', 'gy')
All inputs are finite; a program needn't handle non-finite values.
Results may differ from a plain program's by a relative error of at most 0.0086.
Values may be sent and summed in bfloat16 or wider, within the bound.
A program may use at most 64 MiB of HBM per device.

v0:
```python
import jax
import jax.numpy as jnp
from jax import lax
from jax.sharding import PartitionSpec as P

CHI = 16


def from_behind(x, axis, by):
    length = lax.axis_size(axis)
    return lax.ppermute(x, axis, [(i, (i + by) % length) for i in range(length)])


def split_block(tensors, tests):
    width_count = tensors.shape[0]
    height_count = tensors.shape[1]
    count = width_count * height_count
    flat_tensors = tensors.reshape(count, CHI * CHI, CHI * CHI)
    flat_tests = tests.reshape(count, CHI, CHI * CHI)
    sketch = jnp.einsum(
        "sij,skj->sik", flat_tensors, flat_tests, preferred_element_type=jnp.float32
    )
    gram_matrix = jnp.einsum("sik,sil->skl", sketch, sketch, precision=lax.Precision.HIGHEST)
    lower_factor = jnp.linalg.cholesky(gram_matrix)
    basis = jax.scipy.linalg.solve_triangular(
        lower_factor, jnp.swapaxes(sketch, 1, 2), lower=True
    ).astype(jnp.bfloat16)
    second = jnp.einsum(
        "ski,sij->skj", basis, flat_tensors, preferred_element_type=jnp.float32
    ).astype(jnp.bfloat16)
    shape_out = (width_count, height_count, CHI, CHI * CHI)
    return (basis.reshape(shape_out), second.reshape(shape_out))


def pick_sites(field):
    width_count = field.shape[0]
    height_count = field.shape[1]
    grid = field.reshape(width_count // 2, 2, height_count // 2, 2, CHI, CHI * CHI)
    chosen = jnp.stack([grid[:, 0, :, 0], grid[:, 1, :, 1]], axis=2)
    return chosen.reshape(width_count // 2 * height_count, CHI, CHI * CHI)


def contract_sites(north_east, north_west, south_east, south_west):
    count = north_east.shape[0]
    width = CHI * CHI
    low_left = north_east.reshape(count, CHI, CHI, CHI)
    low_right = north_west.reshape(count, CHI, CHI, CHI)
    high_left = south_east.reshape(count, CHI, CHI, CHI)
    high_right = south_west.reshape(count, CHI, CHI, CHI)
    pair_low = jnp.einsum(
        "naur,nbvr->nabuv", low_left, low_right, preferred_element_type=jnp.float32
    ).astype(jnp.bfloat16)
    pair_high = jnp.einsum(
        "ncru,nevr->nceuv", high_left, high_right, preferred_element_type=jnp.float32
    ).astype(jnp.bfloat16)
    pair_low = pair_low.reshape(count, width, width)
    pair_high = pair_high.reshape(count, width, width)
    raw = jnp.einsum("nij,nkj->nik", pair_low, pair_high, preferred_element_type=jnp.float32)
    squares = jnp.sum(raw * raw, axis=(1, 2))
    norm_value = jnp.sqrt(squares + 1e-06)
    row_index = lax.broadcasted_iota(jnp.int32, (width, width), 0)
    col_index = lax.broadcasted_iota(jnp.int32, (width, width), 1)
    trace_mask = (
        (col_index // CHI == row_index % CHI) & (col_index % CHI == row_index // CHI)
    ).astype(jnp.float32)
    traced = jnp.sum(raw * trace_mask[None], axis=(1, 2))
    coarse = (CHI * CHI * raw / norm_value[:, None, None]).astype(jnp.bfloat16)
    return (coarse, jnp.log(norm_value), CHI * traced / norm_value)


def body(site_tensors, test_matrix):
    width_count = site_tensors.shape[0]
    height_count = site_tensors.shape[1]
    column_in = from_behind((site_tensors[0:1], test_matrix[0:1]), "gx", -1)
    wider_tensors = jnp.concatenate([site_tensors, column_in[0]], axis=0)
    wider_tests = jnp.concatenate([test_matrix, column_in[1]], axis=0)
    row_in = from_behind((wider_tensors[:, 0:1], wider_tests[:, 0:1]), "gy", -1)
    block_tensors = jnp.concatenate([wider_tensors, row_in[0]], axis=1)
    block_tests = jnp.concatenate([wider_tests, row_in[1]], axis=1)
    basis_all, second_all = split_block(block_tensors, block_tests)
    north_east = pick_sites(basis_all[:width_count, :height_count])
    north_west = pick_sites(basis_all[1:, :height_count])
    south_east = pick_sites(second_all[:width_count, 1:])
    south_west = pick_sites(second_all[1:, 1:])
    coarse, log_norm, trace = contract_sites(north_east, north_west, south_east, south_west)
    half_width = width_count // 2
    coarse = coarse.reshape(half_width, height_count, CHI * CHI, CHI * CHI)
    return (
        coarse,
        log_norm.reshape(half_width, height_count),
        trace.reshape(half_width, height_count),
    )


def solution(mesh):
    in_specs = (P("gx", "gy", None, None), P("gx", "gy", None, None))
    out_specs = (P("gx", "gy", None, None), P("gx", "gy"), P("gx", "gy"))
    return jax.shard_map(body, mesh=mesh, in_specs=in_specs, out_specs=out_specs, check_vma=False)
```

profile of v0, /device:TPU:0, one launch (start us, length us, event | category | flops | bytes accessed | tf_op | source)
XLA Modules:
  0.0 191.5 jit_solution(12945135150234578626)
XLA Ops:
  0.6 1.0 slice.60
  1.6 2.5 %collective-permute-start = (bf16[1,2,256,256]{3,2,1,0:T(8,128)(2,1)S(1)}, bf16[1,2,256,256]{3,2,1,0:T(8,128)(2,1)S(1)}, u32[]{:S(2)}, u32[]{:S(2)}) collective-permute-start(bf16[1,2,256,256]{3,2,1,0:T(8,128)(2,1)S(1)} %slice.60), channel_id=1, source_target_pairs={{0,24},{8,0},{16,8},{24,16},{1,25},{9,1},{17,9},{25,17},{2,26},{10... | collective-permute-start | bytes 786440 | tf_op jit(solution)/shard_map/ppermute | solution.py:11
  4.1 1.8 constant_dynamic-update-slice_fusion.1
  5.8 2.1 %collective-permute-done = bf16[1,2,256,256]{3,2,1,0:T(8,128)(2,1)S(1)} collective-permute-done((bf16[1,2,256,256]{3,2,1,0:T(8,128)(2,1)S(1)}, bf16[1,2,256,256]{3,2,1,0:T(8,128)(2,1)S(1)}, u32[]{:S(2)}, u32[]{:S(2)}) %collective-permute-start) | collective-permute-done | bytes 262176 | tf_op jit(solution)/shard_map/ppermute | solution.py:11
  8.1 4.6 %collective-permute-start.1 = (bf16[9,1,256,256]{3,2,1,0:T(8,128)(2,1)S(1)}, bf16[9,1,256,256]{3,2,1,0:T(8,128)(2,1)S(1)}, u32[]{:S(2)}, u32[]{:S(2)}) collective-permute-start(bf16[9,1,256,256]{3,2,1,0:T(8,128)(2,1)S(1)} %slice.76), channel_id=1, source_target_pairs={{0,7},{1,0},{2,1},{3,2},{4,3},{5,4},{6,5},{7,6},{8,15},{9,8},{10,9... | collective-permute-start | bytes 3538952 | tf_op jit(solution)/shard_map/ppermute | solution.py:11
  12.6 1.6 collective-permute-start.2
  17.1 23.4 %collective-permute-done.3 = bf16[9,1,16,256]{3,2,1,0:T(8,128)(2,1)S(1)} collective-permute-done((bf16[9,1,16,256]{3,2,1,0:T(8,128)(2,1)S(1)}, bf16[9,1,16,256]{3,2,1,0:T(8,128)(2,1)S(1)}, u32[]{:S(2)}, u32[]{:S(2)}) %collective-permute-start.3) | collective-permute-done | bytes 73760 | tf_op jit(solution)/shard_map/ppermute | solution.py:11
  40.8 1.0 fusion.13
  42.6 1.2 fusion.14
  43.9 1.7 copy.60
  45.6 1.8 fusion.7
  47.4 40.9 %custom-call.8 = f32[27,16,16]{2,1,0:T(8,128)} custom-call(f32[27,16,16]{2,1,0:T(8,128)} %fusion.7), custom_call_target="Cholesky" | custom-call | tf_op jit(solution)/shard_map/jit(cholesky)/cholesky | solution.py:24
  88.3 1.0 select_reduce_fusion
  90.7 1.7 select_bitcast_fusion
  92.4 34.8 %custom-call.9 = f32[27,1,16,16]{2,3,1,0:T(8,128)} custom-call(f32[27,1,16,16]{3,2,1,0:T(8,128)} %select_bitcast_fusion), custom_call_target="InvertDiagBlocksLowerTriangular" | custom-call | tf_op jit(solution)/shard_map/jit(_solve_triangular)/vmap()/triangular_solve | solution.py:25
  127.2 1.7 convolution_convert_fusion.1
  130.4 5.6 %convert_bitcast_fusion = bf16[8,16,16,16,16]{3,4,1,2,0:T(8,128)(2,1)} fusion(bf16[8,16,16,16,1]{3,2,1,0,4:T(8,128)(2,1)S(1)} %reshape.240, bf16[8,16,16,16,1]{3,2,1,0,4:T(8,128)(2,1)S(1)} %reshape.239), kind=kOutput, calls=%fused_computation | convolution fusion | flops 17301504 | bytes 1179648 | tf_op jit(solution)/shard_map/ncru,nevr->nceuv/dot_general | solution.py:53
  136.0 11.4 %copy.73 = bf16[8,16,16,16,16]{4,3,2,1,0:T(8,128)(2,1)} copy(bf16[8,16,16,16,16]{3,4,1,2,0:T(8,128)(2,1)} %convert_bitcast_fusion) | data formatting | bytes 2097152 | tf_op jit(solution)/shard_map/convert_element_type | solution.py:55
  147.4 10.1 %reshape.235 = bf16[8,256,256]{2,1,0:T(8,128)(2,1)S(1)} reshape(bf16[8,16,16,16,16]{4,3,2,1,0:T(8,128)(2,1)} %copy.73) | data formatting | bytes 2097152 | tf_op jit(solution)/shard_map/reshape | solution.py:57
  158.4 5.6 %convert_bitcast_fusion.1 = bf16[8,16,16,16,16]{3,4,1,2,0:T(8,128)(2,1)} fusion(bf16[8,16,16,16,1]{3,2,1,0,4:T(8,128)(2,1)S(1)} %reshape.238, bf16[8,16,16,16,1]{3,2,1,0,4:T(8,128)(2,1)S(1)} %reshape.237), kind=kOutput, calls=%fused_computation.1 | convolution fusion | flops 17301504 | bytes 1179648 | tf_op jit(solution)/shard_map/naur,nbvr->nabuv/dot_general | solution.py:50
  164.0 11.4 %copy.68 = bf16[8,16,16,16,16]{4,3,2,1,0:T(8,128)(2,1)} copy(bf16[8,16,16,16,16]{3,4,1,2,0:T(8,128)(2,1)} %convert_bitcast_fusion.1) | data formatting | bytes 2097152 | tf_op jit(solution)/shard_map/convert_element_type | solution.py:52
  175.4 11.1 %reshape.231 = bf16[8,256,256]{2,1,0:T(8,128)(2,1)} reshape(bf16[8,16,16,16,16]{4,3,2,1,0:T(8,128)(2,1)} %copy.68) | data formatting | bytes 2097152 | tf_op jit(solution)/shard_map/reshape | solution.py:56
  186.5 1.8 multiply_reduce_fusion
  189.8 1.7 divide_convert_fusion
  (49 shorter events, 9.1 us)
Async XLA Ops:
  1.6 6.3 %collective-permute-start = (bf16[1,2,256,256]{3,2,1,0:T(8,128)(2,1)S(1)}, bf16[1,2,256,256]{3,2,1,0:T(8,128)(2,1)S(1)}, u32[]{:S(2)}, u32[]{:S(2)}) collective-permute-start(bf16[1,2,256,256]{3,2,1,0:T(8,128)(2,1)S(1)} %slice.60), channel_id=1, source_target_pairs={{0,24},{8,0},{16,8},{24,16},{1,25},{9,1},{17,9},{25,17},{2,26},{10... | collective-permute-start | bytes 786440 | tf_op jit(solution)/shard_map/ppermute | solution.py:11
  5.8 6.8 %copy-start.4 = (bf16[8,2,16,256]{3,2,1,0:T(8,128)(2,1)S(1)}, bf16[8,2,16,256]{3,2,1,0:T(8,128)(2,1)}, u32[]{:S(2)}) copy-start(bf16[8,2,16,256]{3,2,1,0:T(8,128)(2,1)} %param.3) | copy-start | bytes 393220
  8.1 32.4 %collective-permute-start.1 = (bf16[9,1,256,256]{3,2,1,0:T(8,128)(2,1)S(1)}, bf16[9,1,256,256]{3,2,1,0:T(8,128)(2,1)S(1)}, u32[]{:S(2)}, u32[]{:S(2)}) collective-permute-start(bf16[9,1,256,256]{3,2,1,0:T(8,128)(2,1)S(1)} %slice.76), channel_id=1, source_target_pairs={{0,7},{1,0},{2,1},{3,2},{4,3},{5,4},{6,5},{7,6},{8,15},{9,8},{10,9... | collective-permute-start | bytes 3538952 | tf_op jit(solution)/shard_map/ppermute | solution.py:11
  12.6 3.2 %collective-permute-start.2 = (bf16[1,2,16,256]{3,2,1,0:T(8,128)(2,1)S(1)}, bf16[1,2,16,256]{3,2,1,0:T(8,128)(2,1)S(1)}, u32[]{:S(2)}, u32[]{:S(2)}) collective-permute-start(bf16[1,2,16,256]{3,2,1,0:T(8,128)(2,1)S(1)} %slice.62), channel_id=1, source_target_pairs={{0,24},{8,0},{16,8},{24,16},{1,25},{9,1},{17,9},{25,17},{2,26},{10... | collective-permute-start | bytes 49160 | tf_op jit(solution)/shard_map/ppermute | solution.py:11
  15.9 24.6 %collective-permute-start.3 = (bf16[9,1,16,256]{3,2,1,0:T(8,128)(2,1)S(1)}, bf16[9,1,16,256]{3,2,1,0:T(8,128)(2,1)S(1)}, u32[]{:S(2)}, u32[]{:S(2)}) collective-permute-start(bf16[9,1,16,256]{3,2,1,0:T(8,128)(2,1)S(1)} %slice.77), channel_id=1, source_target_pairs={{0,7},{1,0},{2,1},{3,2},{4,3},{5,4},{6,5},{7,6},{8,15},{9,8},{10,9... | collective-permute-start | bytes 221192 | tf_op jit(solution)/shard_map/ppermute | solution.py:11
  41.9 0.8 copy-start
  128.9 0.7 copy-start.1
  147.4 10.1 %copy-start.2 = (bf16[27,16,256]{2,1,0:T(8,128)(2,1)S(1)}, bf16[27,16,256]{2,1,0:T(8,128)(2,1)}, u32[]{:S(2)}) copy-start(bf16[27,16,256]{2,1,0:T(8,128)(2,1)} %copy-done.1) | copy-start | bytes 663556
  175.4 11.1 %copy-start.3 = (f32[256,256]{1,0:T(8,128)S(1)}, f32[256,256]{1,0:T(8,128)}, u32[]{:S(2)}) copy-start(f32[256,256]{1,0:T(8,128)} %fusion.5) | copy-start | bytes 786436
where the time goes:
time: 193 us; the launch traced here: 192 us
  other arithmetic  85.2 us (44%)
  local copies, waits for them, and re-layouts  53.2 us (28%)
  waiting for transfers between devices  25.5 us (13%)
  matrix products  17.5 us (9%)
  starting transfers between devices  9.25 us (5%)
    another operation x4, other arithmetic, split_block(): lower_factor = jnp.linalg.cholesky(gram_matrix)  43.2 us
    another operation x3, other arithmetic, split_block(): jax.scipy.linalg.solve_triangular(lower_factor, jnp.swapaxes(sketch, 1, 2...  37.1 us
    ppermute x4, waiting for transfers between devices, from_behind(): lax.ppermute(x, axis, [(i, (i + by) % length) for i in range(length)])  25.5 us
    convert_element_type x1, local copies, waits for them, and re-layouts, contract_sites(): pair_high = jnp.einsum('ncru,nevr->nceuv', high_left, high_right, preferr...  11.4 us
    convert_element_type x1, local copies, waits for them, and re-layouts, contract_sites(): pair_low = jnp.einsum('naur,nbvr->nabuv', low_left, low_right, preferred_...  11.4 us
    reshape x1, local copies, waits for them, and re-layouts, contract_sites(): pair_low = pair_low.reshape(count, width, width)  11.1 us
    reshape x1, local copies, waits for them, and re-layouts, contract_sites(): pair_high = pair_high.reshape(count, width, width)  10.1 us
    ppermute x4, starting transfers between devices, from_behind(): lax.ppermute(x, axis, [(i, (i + by) % length) for i in range(length)])  9.25 us
  transfers between devices with their start and end apart: 4, of which 2 were waited for; matrix products, arithmetic and copies ran while one was open for 2% of the time, Pallas kernels for 0%

commit v1 on v0

v1 whole, which is shorter than its diff:
```python
import jax
import jax.numpy as jnp
from jax import lax
from jax.experimental import pallas as pl
from jax.experimental.pallas import tpu as pltpu
from jax.sharding import PartitionSpec as P

CHI = 16
WIDE = CHI * CHI
HALF = WIDE // 2
MESH = pl.DeviceIdType.MESH
F32 = jnp.float32
BF16 = jnp.bfloat16
NT = (((1,), (1,)), ((), ()))
NN = (((1,), (0,)), ((), ()))


def iota(shape, axis):
    return lax.broadcasted_iota(jnp.int32, shape, axis)


def swap_chunks(rows):
    rows = list(rows)
    chunk = iota(rows[0].shape, 1) // CHI
    for step in (4, 2, 1):
        low = (chunk & step) == 0
        for i in range(8):
            if i & step:
                continue
            first, other = rows[i], rows[i + step]
            rows[i] = jnp.where(low, first, pltpu.roll(other, CHI * step, 1))
            rows[i + step] = jnp.where(low, pltpu.roll(first, HALF - CHI * step, 1), other)
    return rows


def spread(halves):
    parts = []
    for side in range(2):
        parts += swap_chunks([h[:, side * HALF:(side + 1) * HALF].astype(F32) for h in halves])
    return jnp.concatenate(parts, axis=0).astype(BF16)


def regroup(x):
    columns = []
    for upper in range(2):
        column = []
        for side in range(2):
            column += swap_chunks([
                x[(upper * 8 + v) * CHI:(upper * 8 + v + 1) * CHI, side * HALF:(side + 1) * HALF]
                for v in range(8)
            ])
        columns.append(jnp.concatenate(column, axis=0).astype(BF16))
    return jnp.concatenate(columns, axis=1)


def eliminate(gram):
    row = iota(gram.shape, 0)
    lane = iota(gram.shape, 1)
    inverse = jnp.where(row == lane % CHI, 1.0, 0.0).astype(F32)
    pivots = gram
    for k in range(CHI):
        column = jnp.take_along_axis(gram, lane // CHI * CHI + k, axis=1)
        pivot = column[k:k + 1, :]
        pivots = jnp.where(row == k, pivot, pivots)
        factor = jnp.where(row > k, column * (1.0 / pivot), 0.0)
        inverse = inverse - factor * inverse[k:k + 1, :]
        gram = gram - factor * gram[k:k + 1, :]
    return inverse * lax.rsqrt(pivots)


def kernel(
    nx, ny, tensors_ref, tests_ref, coarse_ref, log_ref, trace_ref,
    held, basis_ref, low_ref, up_ref, halo_basis, halo_second, pair_a, pair_b, stage,
    in_sem, out_sem, send_sem, recv_sem,
):
    mx, my = lax.axis_index("gx"), lax.axis_index("gy")
    right, left = lax.rem(mx + 1, nx), lax.rem(mx + nx - 1, nx)
    above, below = lax.rem(my + 1, ny), lax.rem(my + ny - 1, ny)
    loads = [
        pltpu.make_async_copy(tensors_ref.at[pl.ds(2 * c, 2)], held.at[pl.ds(2 * c, 2)], in_sem.at[c])
        for c in range(4)
    ]
    for load in loads:
        load.start()
    barrier = pltpu.get_barrier_semaphore()
    for target in ((right, my), (mx, above), (right, above)):
        pl.semaphore_signal(barrier, inc=1, device_id=target, device_id_type=MESH)

    sketches = []
    for x in range(8):
        if x % 2 == 0:
            loads[x // 2].wait()
        for y in range(2):
            sketches.append(lax.dot_general(tests_ref[x, y], held[x, y], NT, preferred_element_type=F32))
    sketch = jnp.concatenate(sketches, axis=0)
    inverses = []
    for side in range(2):
        part = sketch[side * HALF:(side + 1) * HALF]
        product = lax.dot_general(part, part, NT, precision=lax.Precision.HIGHEST, preferred_element_type=F32)
        chunk = iota((CHI, HALF), 1) // CHI
        gram = jnp.zeros((CHI, HALF), F32)
        for n in range(8):
            gram = gram + jnp.where(chunk == n, product[n * CHI:(n + 1) * CHI], 0.0)
        inverse = eliminate(gram)
        block = jnp.concatenate([jnp.where(chunk == n, inverse, 0.0) for n in range(8)], axis=0)
        basis = lax.dot_general(block, part, NN, precision=lax.Precision.HIGHEST, preferred_element_type=F32)
        basis_ref[pl.ds(8 * side, 8)] = basis.astype(BF16).reshape(8, CHI, WIDE)

    pl.semaphore_wait(barrier, 3)
    copies = [
        pltpu.make_async_remote_copy(
            basis_ref.at[1], halo_basis.at[0], send_sem.at[0], recv_sem.at[0],
            device_id=(left, my), device_id_type=MESH),
        pltpu.make_async_remote_copy(
            low_ref.at[0], halo_second.at[7], send_sem.at[1], recv_sem.at[1],
            device_id=(left, below), device_id_type=MESH),
        pltpu.make_async_remote_copy(
            low_ref.at[pl.ds(1, 7)], halo_second.at[pl.ds(0, 7)], send_sem.at[2], recv_sem.at[2],
            device_id=(mx, below), device_id_type=MESH),
    ]
    copies[0].start()
    for x in range(8):
        low_ref[x] = jnp.dot(basis_ref[2 * x], held[x, 0], preferred_element_type=F32).astype(BF16)
        if x == 0:
            copies[1].start()
    copies[2].start()
    for x in range(8):
        up_ref[x] = jnp.dot(basis_ref[2 * x + 1], held[x, 1], preferred_element_type=F32).astype(BF16)

    flip = (iota((WIDE, WIDE), 0) // CHI == iota((WIDE, WIDE), 1) % CHI) & (
        iota((WIDE, WIDE), 0) % CHI == iota((WIDE, WIDE), 1) // CHI)
    flip_wide = jnp.where(flip, 1.0, 0.0).astype(F32)
    flip_matrix = flip_wide.astype(BF16)
    at_row, at_col = iota((8, 128), 0), iota((8, 128), 1)

    def outgoing(p, g):
        return pltpu.make_async_copy(stage.at[p, g], coarse_ref.at[p, g], out_sem.at[p, g])

    def contract(g, north_east, north_west, south_east, south_west, sums):
        turned = jnp.dot(jnp.concatenate(south_east, axis=0), flip_matrix, preferred_element_type=F32)
        turned = [turned[q * CHI:(q + 1) * CHI] for q in range(4)]
        left_side = spread(north_east + turned)
        left_side = jnp.dot(flip_matrix, left_side, preferred_element_type=F32).astype(BF16)
        right_side = spread(north_west + south_west)
        pair_a[...] = left_side
        pair_b[...] = right_side

        def plaquette(p, sums):
            squares, traces = sums
            chunk = iota((WIDE, HALF), 1) // CHI
            pairs = []
            for q in (p, p + 4):
                masked = jnp.where(chunk == q, pair_b[...], jnp.zeros((), BF16))
                x = lax.dot_general(masked, pair_a[...], NT, preferred_element_type=F32)
                pairs.append(regroup(x))
            raw = lax.dot_general(pairs[0], pairs[1], NT, preferred_element_type=F32)
            square = jnp.sum(jnp.sum(raw * raw, axis=0, keepdims=True), axis=1, keepdims=True) + 1e-6
            traced = jnp.sum(jnp.sum(raw * flip_wide, axis=0, keepdims=True), axis=1, keepdims=True)
            stage[p, g] = (raw * (WIDE * lax.rsqrt(square))).astype(BF16)
            outgoing(p, g).start()
            here = (at_row == p) & (at_col == g)
            return jnp.where(here, square, squares), jnp.where(here, traced, traces)

        return lax.fori_loop(0, 4, plaquette, sums)

    sums = (jnp.ones((8, 128), F32), jnp.zeros((8, 128), F32))
    sums = contract(
        0,
        [basis_ref[4 * p] for p in range(4)],
        [basis_ref[4 * p + 2] for p in range(4)],
        [up_ref[2 * p] for p in range(4)],
        [up_ref[2 * p + 1] for p in range(4)],
        sums,
    )
    for copy in copies:
        copy.wait()
    sums = contract(
        1,
        [basis_ref[4 * p + 3] for p in range(4)],
        [basis_ref[4 * p + 5] for p in range(3)] + [halo_basis[0]],
        [halo_second[2 * p] for p in range(4)],
        [halo_second[2 * p + 1] for p in range(4)],
        sums,
    )
    norm = jnp.sqrt(sums[0])
    log_ref[...] = jnp.log(norm)[:4, :2]
    trace_ref[...] = (CHI * sums[1] / norm)[:4, :2]
    for g in range(2):
        for p in range(4):
            outgoing(p, g).wait()


def solution(mesh):
    nx, ny = mesh.shape["gx"], mesh.shape["gy"]

    def body(site_tensors, test_matrix):
        vmem = pl.BlockSpec(memory_space=pltpu.VMEM)
        anywhere = pl.BlockSpec(memory_space=pl.ANY)
        return pl.pallas_call(
            lambda *refs: kernel(nx, ny, *refs),
            out_shape=(
                jax.ShapeDtypeStruct((4, 2, WIDE, WIDE), BF16),
                jax.ShapeDtypeStruct((4, 2), F32),
                jax.ShapeDtypeStruct((4, 2), F32),
            ),
            in_specs=[anywhere, vmem],
            out_specs=(anywhere, vmem, vmem),
            scratch_shapes=[
                pltpu.VMEM((8, 2, WIDE, WIDE), BF16),
                pltpu.VMEM((16, CHI, WIDE), BF16),
                pltpu.VMEM((8, CHI, WIDE), BF16),
                pltpu.VMEM((8, CHI, WIDE), BF16),
                pltpu.VMEM((1, CHI, WIDE), BF16),
                pltpu.VMEM((8, CHI, WIDE), BF16),
                pltpu.VMEM((WIDE, HALF), BF16),
                pltpu.VMEM((WIDE, HALF), BF16),
                pltpu.VMEM((4, 2, WIDE, WIDE), BF16),
                pltpu.SemaphoreType.DMA((4,)),
                pltpu.SemaphoreType.DMA((4, 2)),
                pltpu.SemaphoreType.DMA((3,)),
                pltpu.SemaphoreType.DMA((3,)),
            ],
            compiler_params=pltpu.CompilerParams(
                collective_id=0, has_side_effects=True, vmem_limit_bytes=32 * 2**20),
            cost_estimate=pl.CostEstimate(
                flops=1_000_000_000, bytes_accessed=4_000_000, transcendentals=0),
        )(site_tensors, test_matrix)

    in_specs = (P("gx", "gy", None, None), P("gx", "gy", None, None))
    out_specs = (P("gx", "gy", None, None), P("gx", "gy"), P("gx", "gy"))
    return jax.shard_map(body, mesh=mesh, in_specs=in_specs, out_specs=out_specs, check_vma=False)
```

time: 193 us -> 22.2 us (0.12)
  other arithmetic: 85.2 us -> 0 us
  local copies, waits for them, and re-layouts: 53.2 us -> 4.75 us
  waiting for transfers between devices: 25.5 us -> 0 us
  matrix products: 17.5 us -> 0 us
  Pallas kernels: 0 us -> 16.6 us
  starting transfers between devices: 9.25 us -> 0 us
    another operation x11 -> x0, other arithmetic: 80.4 us -> none  [the longest x4 43.2 us: split_block(): lower_factor = jnp.linalg.cholesky(gram_matrix)]
    ppermute x4 -> x0, waiting for transfers between devices: 25.5 us -> none  [from_behind(): lax.ppermute(x, axis, [(i, (i + by) % length) for i in range(length)])]
    convert_element_type x2 -> x0, local copies, waits for them, and re-layouts: 22.9 us -> none  [the longest x1 11.4 us: contract_sites(): pair_high = jnp.einsum('ncru,nevr->nceuv', high_left, high_right, preferr...]
    reshape x2 -> x0, local copies, waits for them, and re-layouts: 21.2 us -> none  [the longest x1 11.1 us: contract_sites(): pair_low = pair_low.reshape(count, width, width)]
    pallas_call x0 -> x1, Pallas kernels: none -> 16.6 us  [body(): pl.pallas_call(lambda *refs: kernel(nx, ny, *refs), out_shape=(jax.ShapeD...]
    dot_general x6 -> x0, matrix products: 15.8 us -> none  [the longest x1 5.58 us: contract_sites(): jnp.einsum('naur,nbvr->nabuv', low_left, low_right, preferred_element_typ...]
    ppermute x4 -> x0, starting transfers between devices: 9.25 us -> none  [from_behind(): lax.ppermute(x, axis, [(i, (i + by) % length) for i in range(length)])]
    convert_element_type x2 -> x0, other arithmetic: 2.68 us -> none  [the longest x1 1.71 us: contract_sites(): coarse = (CHI * CHI * raw / norm_value[:, None, None]).astype(jnp.bfloat16)]
  transfers between devices with their start and end apart: 4 -> 0, of which waited for: 2 -> 0; matrix products, arithmetic and copies ran while one was open for 2% -> 0% of each run, Pallas kernels for 0% -> 0%
where the time goes in v1:
time: 22.2 us; the launch traced here: 22 us
  Pallas kernels  16.6 us (75%)
  local copies, waits for them, and re-layouts  4.75 us (21%)
  between operations  0.65 us (3%)
    pallas_call x1, Pallas kernels, body(): pl.pallas_call(lambda *refs: kernel(nx, ny, *refs), out_shape=(jax.ShapeD...  16.6 us
    unnamed x5, local copies, waits for them, and re-layouts  3.46 us
    pallas_call x2, local copies, waits for them, and re-layouts, body(): pl.pallas_call(lambda *refs: kernel(nx, ny, *refs), out_shape=(jax.ShapeD...  1.3 us

profile of v1, /device:TPU:0, one launch (start us, length us, event | category | flops | bytes accessed | tf_op | source)
XLA Modules:
  0.0 22.0 jit_solution(14838918060510709193)
XLA Ops:
  0.6 0.0 copy-start
  0.6 1.6 %copy-done = bf16[8,2,256,256]{3,2,1,0:T(8,128)(2,1)S(1)} copy-done((bf16[8,2,256,256]{3,2,1,0:T(8,128)(2,1)S(1)}, bf16[8,2,256,256]{3,2,1,0:T(8,128)(2,1)}, u32[]{:S(2)}) %copy-start) | copy-done | bytes 2097176
  2.2 0.0 copy-start.1
  2.2 0.9 %copy-done.1 = bf16[8,2,16,256]{3,2,1,0:T(8,128)(2,1)S(1)} copy-done((bf16[8,2,16,256]{3,2,1,0:T(8,128)(2,1)S(1)}, bf16[8,2,16,256]{3,2,1,0:T(8,128)(2,1)}, u32[]{:S(2)}) %copy-start.1) | copy-done | bytes 131096
  3.1 16.6 %shard_map.49 = (bf16[4,2,256,256]{3,2,1,0:T(8,128)(2,1)S(1)}, f32[4,2]{1,0:T(4,128)S(1)}, f32[4,2]{1,0:T(4,128)S(1)}) custom-call(bf16[8,2,256,256]{3,2,1,0:T(8,128)(2,1)S(1)} %copy-done, bf16[8,2,16,256]{3,2,1,0:T(8,128)(2,1)S(1)} %copy-done.1), custom_call_target="tpu_custom_call" | custom-call | flops 1000000000 | bytes 4000000 | tf_op jit(solution)/shard_map/pallas_call | solution.py:199
  19.8 0.6 %copy.5 = f32[4,2]{0,1:T(2,128)} copy(f32[4,2]{1,0:T(4,128)S(1)} %get-tuple-element.4) | data formatting | bytes 64 | tf_op jit(solution)/shard_map/pallas_call | solution.py:199
  20.4 0.6 %copy.6 = f32[4,2]{0,1:T(2,128)} copy(f32[4,2]{1,0:T(4,128)S(1)} %get-tuple-element.5) | data formatting | bytes 64 | tf_op jit(solution)/shard_map/pallas_call | solution.py:199
  21.1 1.0 %copy.8 = bf16[4,2,256,256]{3,2,1,0:T(8,128)(2,1)} copy(bf16[4,2,256,256]{3,2,1,0:T(8,128)(2,1)S(1)} %get-tuple-element.9) | data formatting | bytes 2097152
Async XLA Ops:
  0.6 1.6 %copy-start = (bf16[8,2,256,256]{3,2,1,0:T(8,128)(2,1)S(1)}, bf16[8,2,256,256]{3,2,1,0:T(8,128)(2,1)}, u32[]{:S(2)}) copy-start(bf16[8,2,256,256]{3,2,1,0:T(8,128)(2,1)} %refs_0_.1) | copy-start | bytes 6291460
  2.2 0.9 %copy-start.1 = (bf16[8,2,16,256]{3,2,1,0:T(8,128)(2,1)S(1)}, bf16[8,2,16,256]{3,2,1,0:T(8,128)(2,1)}, u32[]{:S(2)}) copy-start(bf16[8,2,16,256]{3,2,1,0:T(8,128)(2,1)} %refs_1_.1) | copy-start | bytes 393220

commit v2 on v1

--- a/solution.py
+++ b/solution.py
@@ -36,8 +36,8 @@
 def spread(halves):
     parts = []
     for side in range(2):
-        parts += swap_chunks([h[:, side * HALF:(side + 1) * HALF].astype(F32) for h in halves])
-    return jnp.concatenate(parts, axis=0).astype(BF16)
+        parts += swap_chunks([h[:, side * HALF:(side + 1) * HALF] for h in halves])
+    return jnp.concatenate(parts, axis=0)
 
 
 def regroup(x):
@@ -49,59 +49,62 @@
                 x[(upper * 8 + v) * CHI:(upper * 8 + v + 1) * CHI, side * HALF:(side + 1) * HALF]
                 for v in range(8)
             ])
-        columns.append(jnp.concatenate(column, axis=0).astype(BF16))
+        columns.append(jnp.concatenate(column, axis=0))
     return jnp.concatenate(columns, axis=1)
 
 
-def eliminate(gram):
-    row = iota(gram.shape, 0)
-    lane = iota(gram.shape, 1)
-    inverse = jnp.where(row == lane % CHI, 1.0, 0.0).astype(F32)
-    pivots = gram
+def eliminate(grams):
+    row = iota(grams[0].shape, 0)
+    lane = iota(grams[0].shape, 1)
+    grams = list(grams)
+    inverses = [jnp.where(row == lane % CHI, 1.0, 0.0).astype(F32)] * len(grams)
+    pivots = list(grams)
     for k in range(CHI):
-        column = jnp.take_along_axis(gram, lane // CHI * CHI + k, axis=1)
-        pivot = column[k:k + 1, :]
-        pivots = jnp.where(row == k, pivot, pivots)
-        factor = jnp.where(row > k, column * (1.0 / pivot), 0.0)
-        inverse = inverse - factor * inverse[k:k + 1, :]
-        gram = gram - factor * gram[k:k + 1, :]
-    return inverse * lax.rsqrt(pivots)
+        for s in range(len(grams)):
+            column = jnp.take_along_axis(grams[s], lane // CHI * CHI + k, axis=1)
+            pivot = column[k:k + 1, :]
+            pivots[s] = jnp.where(row == k, pivot, pivots[s])
+            factor = jnp.where(row > k, column * (1.0 / pivot), 0.0)
+            inverses[s] = inverses[s] - factor * inverses[s][k:k + 1, :]
+            grams[s] = grams[s] - factor * grams[s][k:k + 1, :]
+    return [i * lax.rsqrt(p) for i, p in zip(inverses, pivots)]
 
 
 def kernel(
     nx, ny, tensors_ref, tests_ref, coarse_ref, log_ref, trace_ref,
     held, basis_ref, low_ref, up_ref, halo_basis, halo_second, pair_a, pair_b, stage,
-    in_sem, out_sem, send_sem, recv_sem,
+    tests, in_sem, out_sem, send_sem, recv_sem,
 ):
     mx, my = lax.axis_index("gx"), lax.axis_index("gy")
     right, left = lax.rem(mx + 1, nx), lax.rem(mx + nx - 1, nx)
     above, below = lax.rem(my + 1, ny), lax.rem(my + ny - 1, ny)
-    loads = [
-        pltpu.make_async_copy(tensors_ref.at[pl.ds(2 * c, 2)], held.at[pl.ds(2 * c, 2)], in_sem.at[c])
-        for c in range(4)
-    ]
-    for load in loads:
+    loads = [pltpu.make_async_copy(tensors_ref.at[c], held.at[c], in_sem.at[c]) for c in range(8)]
+    loads.append(pltpu.make_async_copy(tests_ref, tests, in_sem.at[8]))
+    loads[8].start()
+    for load in loads[:8]:
         load.start()
     barrier = pltpu.get_barrier_semaphore()
     for target in ((right, my), (mx, above), (right, above)):
         pl.semaphore_signal(barrier, inc=1, device_id=target, device_id_type=MESH)
 
     sketches = []
+    loads[8].wait()
     for x in range(8):
-        if x % 2 == 0:
-            loads[x // 2].wait()
+        loads[x].wait()
         for y in range(2):
-            sketches.append(lax.dot_general(tests_ref[x, y], held[x, y], NT, preferred_element_type=F32))
+            sketches.append(lax.dot_general(tests[x, y], held[x, y], NT, preferred_element_type=F32))
     sketch = jnp.concatenate(sketches, axis=0)
-    inverses = []
+    chunk = iota((CHI, HALF), 1) // CHI
+    grams = []
     for side in range(2):
         part = sketch[side * HALF:(side + 1) * HALF]
         product = lax.dot_general(part, part, NT, precision=lax.Precision.HIGHEST, preferred_element_type=F32)
-        chunk = iota((CHI, HALF), 1) // CHI
         gram = jnp.zeros((CHI, HALF), F32)
         for n in range(8):
             gram = gram + jnp.where(chunk == n, product[n * CHI:(n + 1) * CHI], 0.0)
-        inverse = eliminate(gram)
+        grams.append(gram)
+    for side, inverse in enumerate(eliminate(grams)):
+        part = sketch[side * HALF:(side + 1) * HALF]
         block = jnp.concatenate([jnp.where(chunk == n, inverse, 0.0) for n in range(8)], axis=0)
         basis = lax.dot_general(block, part, NN, precision=lax.Precision.HIGHEST, preferred_element_type=F32)
         basis_ref[pl.ds(8 * side, 8)] = basis.astype(BF16).reshape(8, CHI, WIDE)
@@ -137,7 +140,7 @@
         return pltpu.make_async_copy(stage.at[p, g], coarse_ref.at[p, g], out_sem.at[p, g])
 
     def contract(g, north_east, north_west, south_east, south_west, sums):
-        turned = jnp.dot(jnp.concatenate(south_east, axis=0), flip_matrix, preferred_element_type=F32)
+        turned = jnp.dot(jnp.concatenate(south_east, axis=0), flip_matrix, preferred_element_type=F32).astype(BF16)
         turned = [turned[q * CHI:(q + 1) * CHI] for q in range(4)]
         left_side = spread(north_east + turned)
         left_side = jnp.dot(flip_matrix, left_side, preferred_element_type=F32).astype(BF16)
@@ -145,14 +148,18 @@
         pair_a[...] = left_side
         pair_b[...] = right_side
 
-        def plaquette(p, sums):
-            squares, traces = sums
-            chunk = iota((WIDE, HALF), 1) // CHI
+        chunk = iota((WIDE, HALF), 1) // CHI
+
+        def paired(p):
             pairs = []
             for q in (p, p + 4):
                 masked = jnp.where(chunk == q, pair_b[...], jnp.zeros((), BF16))
                 x = lax.dot_general(masked, pair_a[...], NT, preferred_element_type=F32)
-                pairs.append(regroup(x))
+                pairs.append(regroup(x.astype(BF16)))
+            return pairs
+
+        def finish(p, pairs, sums):
+            squares, traces = sums
             raw = lax.dot_general(pairs[0], pairs[1], NT, preferred_element_type=F32)
             square = jnp.sum(jnp.sum(raw * raw, axis=0, keepdims=True), axis=1, keepdims=True) + 1e-6
             traced = jnp.sum(jnp.sum(raw * flip_wide, axis=0, keepdims=True), axis=1, keepdims=True)
@@ -161,7 +168,11 @@
             here = (at_row == p) & (at_col == g)
             return jnp.where(here, square, squares), jnp.where(here, traced, traces)
 
-        return lax.fori_loop(0, 4, plaquette, sums)
+        ahead = paired(0)
+        for p in range(4):
+            pairs, ahead = ahead, paired(p + 1) if p < 3 else None
+            sums = finish(p, pairs, sums)
+        return sums
 
     sums = (jnp.ones((8, 128), F32), jnp.zeros((8, 128), F32))
     sums = contract(
@@ -195,7 +206,7 @@
 
     def body(site_tensors, test_matrix):
         vmem = pl.BlockSpec(memory_space=pltpu.VMEM)
-        anywhere = pl.BlockSpec(memory_space=pl.ANY)
+        hbm = pl.BlockSpec(memory_space=pltpu.HBM)
         return pl.pallas_call(
             lambda *refs: kernel(nx, ny, *refs),
             out_shape=(
@@ -203,8 +214,8 @@
                 jax.ShapeDtypeStruct((4, 2), F32),
                 jax.ShapeDtypeStruct((4, 2), F32),
             ),
-            in_specs=[anywhere, vmem],
-            out_specs=(anywhere, vmem, vmem),
+            in_specs=[hbm, hbm],
+            out_specs=(hbm, vmem, vmem),
             scratch_shapes=[
                 pltpu.VMEM((8, 2, WIDE, WIDE), BF16),
                 pltpu.VMEM((16, CHI, WIDE), BF16),
@@ -215,13 +226,14 @@
                 pltpu.VMEM((WIDE, HALF), BF16),
                 pltpu.VMEM((WIDE, HALF), BF16),
                 pltpu.VMEM((4, 2, WIDE, WIDE), BF16),
-                pltpu.SemaphoreType.DMA((4,)),
+                pltpu.VMEM((8, 2, CHI, WIDE), BF16),
+                pltpu.SemaphoreType.DMA((9,)),
                 pltpu.SemaphoreType.DMA((4, 2)),
                 pltpu.SemaphoreType.DMA((3,)),
                 pltpu.SemaphoreType.DMA((3,)),
             ],
             compiler_params=pltpu.CompilerParams(
-                collective_id=0, has_side_effects=True, vmem_limit_bytes=32 * 2**20),
+                collective_id=0, has_side_effects=True, vmem_limit_bytes=63 * 2**20),
             cost_estimate=pl.CostEstimate(
                 flops=1_000_000_000, bytes_accessed=4_000_000, transcendentals=0),
         )(site_tensors, test_matrix)

time: 22.2 us -> 19.4 us (0.87)
  Pallas kernels: 16.6 us -> 13.7 us
    pallas_call x1, Pallas kernels: 16.6 us -> 13.7 us  [body(): pl.pallas_call(lambda *refs: kernel(nx, ny, *refs), out_shape=(jax.ShapeD...]
    pallas_call x2, local copies, waits for them, and re-layouts: 1.3 us -> 2.62 us  [body(): pl.pallas_call(lambda *refs: kernel(nx, ny, *refs), out_shape=(jax.ShapeD...]
    unnamed x5 -> x1, local copies, waits for them, and re-layouts: 3.46 us -> 2.26 us
where the time goes in v2:
time: 19.4 us; the launch traced here: 19.2 us
  Pallas kernels  13.7 us (71%)
  local copies, waits for them, and re-layouts  4.88 us (25%)
  between operations  0.64 us (3%)
    pallas_call x1, Pallas kernels, body(): pl.pallas_call(lambda *refs: kernel(nx, ny, *refs), out_shape=(jax.ShapeD...  13.7 us
    pallas_call x2, local copies, waits for them, and re-layouts, body(): pl.pallas_call(lambda *refs: kernel(nx, ny, *refs), out_shape=(jax.ShapeD...  2.62 us
    unnamed x1, local copies, waits for them, and re-layouts  2.26 us

profile of v2, /device:TPU:0, one launch (start us, length us, event | category | flops | bytes accessed | tf_op | source)
XLA Modules:
  0.0 19.2 jit_solution(15715812418336382876)
XLA Ops:
  0.6 13.7 %shard_map.49 = (bf16[4,2,256,256]{3,2,1,0:T(8,128)(2,1)}, f32[4,2]{1,0:T(4,128)}, f32[4,2]{1,0:T(4,128)}) custom-call(bf16[8,2,256,256]{3,2,1,0:T(8,128)(2,1)} %refs_0_.1, bf16[8,2,16,256]{3,2,1,0:T(8,128)(2,1)} %refs_1_.1), custom_call_target="tpu_custom_call" | custom-call | flops 1000000000 | bytes 4000000 | tf_op jit(solution)/shard_map/pallas_call | solution.py:210
  14.3 1.3 %copy.5 = f32[4,2]{0,1:T(2,128)} copy(f32[4,2]{1,0:T(4,128)} %get-tuple-element.4) | data formatting | bytes 64 | tf_op jit(solution)/shard_map/pallas_call | solution.py:210
  15.6 1.3 %copy.6 = f32[4,2]{0,1:T(2,128)} copy(f32[4,2]{1,0:T(4,128)} %get-tuple-element.5) | data formatting | bytes 64 | tf_op jit(solution)/shard_map/pallas_call | solution.py:210
  16.9 2.3 %copy.8 = bf16[4,2,256,256]{3,2,1,0:T(8,128)(2,1)} copy(bf16[4,2,256,256]{3,2,1,0:T(8,128)(2,1)} %get-tuple-element.9) | data formatting | bytes 2097152

commit v3 on v2

--- a/solution.py
+++ b/solution.py
@@ -70,10 +70,48 @@
     return [i * lax.rsqrt(p) for i, p in zip(inverses, pivots)]
 
 
-def kernel(
-    nx, ny, tensors_ref, tests_ref, coarse_ref, log_ref, trace_ref,
-    held, basis_ref, low_ref, up_ref, halo_basis, halo_second, pair_a, pair_b, stage,
-    tests, in_sem, out_sem, send_sem, recv_sem,
+def flip_mask():
+    row, col = iota((WIDE, WIDE), 0), iota((WIDE, WIDE), 1)
+    return jnp.where((row // CHI == col % CHI) & (row % CHI == col // CHI), 1.0, 0.0).astype(F32)
+
+
+def contract(g, north_east, north_west, south_east, south_west, sums, store):
+    flip_wide = flip_mask()
+    flip_matrix = flip_wide.astype(BF16)
+    at_row, at_col = iota((8, 128), 0), iota((8, 128), 1)
+    chunk = iota((WIDE, HALF), 1) // CHI
+    turned = jnp.dot(jnp.concatenate(south_east, axis=0), flip_matrix, preferred_element_type=F32).astype(BF16)
+    turned = [turned[q * CHI:(q + 1) * CHI] for q in range(4)]
+    left_side = spread(north_east + turned)
+    left_side = jnp.dot(flip_matrix, left_side, preferred_element_type=F32).astype(BF16)
+    right_side = spread(north_west + south_west)
+    left_turned, right_turned = left_side.T, right_side.T
+    zero = jnp.zeros((), BF16)
+
+    def paired(p):
+        low = jnp.dot(jnp.where(chunk == p, right_side, zero), left_turned, preferred_element_type=F32)
+        high = jnp.dot(jnp.where(chunk == p + 4, left_side, zero), right_turned, preferred_element_type=F32)
+        return regroup(low.astype(BF16)), regroup(high.astype(BF16))
+
+    def finish(p, pairs, sums):
+        squares, traces = sums
+        raw = jnp.dot(pairs[0], pairs[1], preferred_element_type=F32)
+        square = jnp.sum(jnp.sum(raw * raw, axis=0, keepdims=True), axis=1, keepdims=True) + 1e-6
+        traced = jnp.sum(jnp.sum(raw * flip_wide, axis=0, keepdims=True), axis=1, keepdims=True)
+        store(p, (raw * (WIDE * lax.rsqrt(square))).astype(BF16))
+        here = (at_row == g) & (at_col == p)
+        return jnp.where(here, square, squares), jnp.where(here, traced, traces)
+
+    ahead = paired(0)
+    for p in range(4):
+        pairs, ahead = ahead, paired(p + 1) if p < 3 else None
+        sums = finish(p, pairs, sums)
+    return sums
+
+
+def split_kernel(
+    nx, ny, tensors_ref, tests_ref, coarse_ref, sums_ref, ne_ref, nw_ref, halo_ref,
+    held, basis_ref, low_ref, up_ref, halo_basis, halo_second, tests, in_sem, send_sem, recv_sem,
 ):
     mx, my = lax.axis_index("gx"), lax.axis_index("gy")
     right, left = lax.rem(mx + 1, nx), lax.rem(mx + nx - 1, nx)
@@ -130,49 +168,8 @@
     for x in range(8):
         up_ref[x] = jnp.dot(basis_ref[2 * x + 1], held[x, 1], preferred_element_type=F32).astype(BF16)
 
-    flip = (iota((WIDE, WIDE), 0) // CHI == iota((WIDE, WIDE), 1) % CHI) & (
-        iota((WIDE, WIDE), 0) % CHI == iota((WIDE, WIDE), 1) // CHI)
-    flip_wide = jnp.where(flip, 1.0, 0.0).astype(F32)
-    flip_matrix = flip_wide.astype(BF16)
-    at_row, at_col = iota((8, 128), 0), iota((8, 128), 1)
-
-    def outgoing(p, g):
-        return pltpu.make_async_copy(stage.at[p, g], coarse_ref.at[p, g], out_sem.at[p, g])
-
-    def contract(g, north_east, north_west, south_east, south_west, sums):
-        turned = jnp.dot(jnp.concatenate(south_east, axis=0), flip_matrix, preferred_element_type=F32).astype(BF16)
-        turned = [turned[q * CHI:(q + 1) * CHI] for q in range(4)]
-        left_side = spread(north_east + turned)
-        left_side = jnp.dot(flip_matrix, left_side, preferred_element_type=F32).astype(BF16)
-        right_side = spread(north_west + south_west)
-        pair_a[...] = left_side
-        pair_b[...] = right_side
-
-        chunk = iota((WIDE, HALF), 1) // CHI
-
-        def paired(p):
-            pairs = []
-            for q in (p, p + 4):
-                masked = jnp.where(chunk == q, pair_b[...], jnp.zeros((), BF16))
-                x = lax.dot_general(masked, pair_a[...], NT, preferred_element_type=F32)
-                pairs.append(regroup(x.astype(BF16)))
-            return pairs
-
-        def finish(p, pairs, sums):
-            squares, traces = sums
-            raw = lax.dot_general(pairs[0], pairs[1], NT, preferred_element_type=F32)
-            square = jnp.sum(jnp.sum(raw * raw, axis=0, keepdims=True), axis=1, keepdims=True) + 1e-6
-            traced = jnp.sum(jnp.sum(raw * flip_wide, axis=0, keepdims=True), axis=1, keepdims=True)
-            stage[p, g] = (raw * (WIDE * lax.rsqrt(square))).astype(BF16)
-            outgoing(p, g).start()
-            here = (at_row == p) & (at_col == g)
-            return jnp.where(here, square, squares), jnp.where(here, traced, traces)
-
-        ahead = paired(0)
-        for p in range(4):
-            pairs, ahead = ahead, paired(p + 1) if p < 3 else None
-            sums = finish(p, pairs, sums)
-        return sums
+    def store(p, value):
+        coarse_ref[p] = value
 
     sums = (jnp.ones((8, 128), F32), jnp.zeros((8, 128), F32))
     sums = contract(
@@ -182,40 +179,65 @@
         [up_ref[2 * p] for p in range(4)],
         [up_ref[2 * p + 1] for p in range(4)],
         sums,
+        store,
     )
+    sums_ref[0] = sums[0]
+    sums_ref[1] = sums[1]
+    for p in range(4):
+        ne_ref[p] = basis_ref[4 * p + 3]
+        if p < 3:
+            nw_ref[p] = basis_ref[4 * p + 5]
     for copy in copies:
         copy.wait()
-    sums = contract(
+    nw_ref[3] = halo_basis[0]
+    halo_ref[...] = halo_second[...]
+
+
+def join_kernel(first_ref, sums_ref, ne_ref, nw_ref, halo_ref, coarse_ref, log_ref, trace_ref, stage, out_sem):
+    early = [pltpu.make_async_copy(first_ref.at[p], coarse_ref.at[p, 0], out_sem.at[p]) for p in range(4)]
+    late = [pltpu.make_async_copy(stage.at[p], coarse_ref.at[p, 1], out_sem.at[4 + p]) for p in range(4)]
+    for copy in early:
+        copy.start()
+
+    def store(p, value):
+        stage[p] = value
+        late[p].start()
+
+    squares, traces = contract(
         1,
-        [basis_ref[4 * p + 3] for p in range(4)],
-        [basis_ref[4 * p + 5] for p in range(3)] + [halo_basis[0]],
-        [halo_second[2 * p] for p in range(4)],
-        [halo_second[2 * p + 1] for p in range(4)],
-        sums,
+        [ne_ref[p] for p in range(4)],
+        [nw_ref[p] for p in range(4)],
+        [halo_ref[2 * p] for p in range(4)],
+        [halo_ref[2 * p + 1] for p in range(4)],
+        (sums_ref[0], sums_ref[1]),
+        store,
     )
-    norm = jnp.sqrt(sums[0])
-    log_ref[...] = jnp.log(norm)[:4, :2]
-    trace_ref[...] = (CHI * sums[1] / norm)[:4, :2]
-    for g in range(2):
-        for p in range(4):
-            outgoing(p, g).wait()
+    norm = jnp.sqrt(squares)
+    log_ref[...] = jnp.log(norm)[:2, :4]
+    trace_ref[...] = (CHI * traces / norm)[:2, :4]
+    for copy in early + late:
+        copy.wait()
 
 
 def solution(mesh):
     nx, ny = mesh.shape["gx"], mesh.shape["gy"]
+    vmem = pl.BlockSpec(memory_space=pltpu.VMEM)
+    hbm = pl.BlockSpec(memory_space=pltpu.HBM)
 
     def body(site_tensors, test_matrix):
-        vmem = pl.BlockSpec(memory_space=pltpu.VMEM)
-        hbm = pl.BlockSpec(memory_space=pltpu.HBM)
-        return pl.pallas_call(
-            lambda *refs: kernel(nx, ny, *refs),
+        site_tensors = pltpu.with_memory_space_constraint(site_tensors, pltpu.HBM)
+        test_matrix = pltpu.with_memory_space_constraint(test_matrix, pltpu.HBM)
+        between = pl.pallas_call(
+            lambda *refs: split_kernel(nx, ny, *refs),
             out_shape=(
-                jax.ShapeDtypeStruct((4, 2, WIDE, WIDE), BF16),
-                jax.ShapeDtypeStruct((4, 2), F32),
-                jax.ShapeDtypeStruct((4, 2), F32),
+                pltpu.VMEM((4, WIDE, WIDE), BF16),
+                pltpu.VMEM((2, 8, 128), F32),
+                pltpu.VMEM((4, CHI, WIDE), BF16),
+                pltpu.VMEM((4, CHI, WIDE), BF16),
+                pltpu.VMEM((8, CHI, WIDE), BF16),
             ),
             in_specs=[hbm, hbm],
-            out_specs=(hbm, vmem, vmem),
+            out_specs=(vmem,) * 5,
             scratch_shapes=[
                 pltpu.VMEM((8, 2, WIDE, WIDE), BF16),
                 pltpu.VMEM((16, CHI, WIDE), BF16),
@@ -223,20 +245,35 @@
                 pltpu.VMEM((8, CHI, WIDE), BF16),
                 pltpu.VMEM((1, CHI, WIDE), BF16),
                 pltpu.VMEM((8, CHI, WIDE), BF16),
-                pltpu.VMEM((WIDE, HALF), BF16),
-                pltpu.VMEM((WIDE, HALF), BF16),
-                pltpu.VMEM((4, 2, WIDE, WIDE), BF16),
                 pltpu.VMEM((8, 2, CHI, WIDE), BF16),
                 pltpu.SemaphoreType.DMA((9,)),
-                pltpu.SemaphoreType.DMA((4, 2)),
                 pltpu.SemaphoreType.DMA((3,)),
                 pltpu.SemaphoreType.DMA((3,)),
             ],
             compiler_params=pltpu.CompilerParams(
-                collective_id=0, has_side_effects=True, vmem_limit_bytes=63 * 2**20),
+                collective_id=0, has_side_effects=True, vmem_limit_bytes=24 * 2**20),
             cost_estimate=pl.CostEstimate(
-                flops=1_000_000_000, bytes_accessed=4_000_000, transcendentals=0),
+                flops=700_000_000, bytes_accessed=3_000_000, transcendentals=0),
         )(site_tensors, test_matrix)
+        between = [pltpu.with_memory_space_constraint(x, pltpu.VMEM) for x in between]
+        coarse, log_norm, trace = pl.pallas_call(
+            join_kernel,
+            out_shape=(
+                pltpu.HBM((4, 2, WIDE, WIDE), BF16),
+                jax.ShapeDtypeStruct((2, 4), F32),
+                jax.ShapeDtypeStruct((2, 4), F32),
+            ),
+            in_specs=[vmem] * 5,
+            out_specs=(hbm, vmem, vmem),
+            scratch_shapes=[
+                pltpu.VMEM((4, WIDE, WIDE), BF16),
+                pltpu.SemaphoreType.DMA((8,)),
+            ],
+            compiler_params=pltpu.CompilerParams(vmem_limit_bytes=24 * 2**20),
+            cost_estimate=pl.CostEstimate(
+                flops=300_000_000, bytes_accessed=1_000_000, transcendentals=0),
+        )(*between)
+        return coarse, log_norm.T, trace.T
 
     in_specs = (P("gx", "gy", None, None), P("gx", "gy", None, None))
     out_specs = (P("gx", "gy", None, None), P("gx", "gy"), P("gx", "gy"))

time: 19.4 us -> 14.4 us (0.74)
  local copies, waits for them, and re-layouts: 4.88 us -> 0 us
    pallas_call x2 -> x0, local copies, waits for them, and re-layouts: 2.62 us -> none  [body(): pl.pallas_call(lambda *refs: kernel(nx, ny, *refs), out_shape=(jax.ShapeD...]
    unnamed x1 -> x0, local copies, waits for them, and re-layouts: 2.26 us -> none
    pallas_call x1 -> x2, Pallas kernels: 13.7 us -> 13.6 us  [the longest x1 10.1 us: body(): pl.pallas_call(lambda *refs: split_kernel(nx, ny, *refs), out_shape=(pltp...]
where the time goes in v3:
time: 14.4 us; the launch traced here: 14.2 us
  Pallas kernels  13.6 us (94%)
  between operations  0.64 us (4%)
    pallas_call x1, Pallas kernels, body(): pl.pallas_call(lambda *refs: split_kernel(nx, ny, *refs), out_shape=(pltp...  10.1 us
    pallas_call x1, Pallas kernels, body(): pl.pallas_call(join_kernel, out_shape=(pltpu.HBM((4, 2, WIDE, WIDE), BF16...  3.48 us

profile of v3, /device:TPU:0, one launch (start us, length us, event | category | flops | bytes accessed | tf_op | source)
XLA Modules:
  0.0 14.2 jit_solution(9944521333437258246)
XLA Ops:
  0.6 10.1 %shard_map.49 = (bf16[4,256,256]{2,1,0:T(8,128)(2,1)S(1)}, f32[2,8,128]{2,1,0:T(8,128)S(1)}, bf16[4,16,256]{2,1,0:T(8,128)(2,1)S(1)}, bf16[4,16,256]{2,1,0:T(8,128)(2,1)S(1)}, bf16[8,16,256]{2,1,0:T(8,128)(2,1)S(1)}) custom-call(bf16[8,2,256,256]{3,2,1,0:T(8,128)(2,1)} %refs_0_.1, bf16[8,2,16,256]{3,2,1,0:T(8,128)(2,1)} %refs_1_.1), custom_call_target="tpu_custom_call" | custom-call | flops 700000000 | bytes 3000000 | tf_op jit(solution)/shard_map/pallas_call | solution.py:230
  10.7 3.5 %shard_map.50 = (bf16[4,2,256,256]{3,2,1,0:T(8,128)(2,1)}, f32[2,4]{1,0:T(2,128)}, f32[2,4]{1,0:T(2,128)}) custom-call(bf16[4,256,256]{2,1,0:T(8,128)(2,1)S(1)} %get-tuple-element.11.first_ref, f32[2,8,128]{2,1,0:T(8,128)S(1)} %get-tuple-element.12.sums_ref, bf16[4,16,256]{2,1,0:T(8,128)(2,1)S(1)} %get-tuple-element.13.ne_ref, ...), custom_call_target="tpu_custom_call" | custom-call | flops 300000000 | bytes 1000000 | tf_op jit(solution)/shard_map/pallas_call | solution.py:259

commit v4 on v3

--- a/solution.py
+++ b/solution.py
@@ -59,14 +59,24 @@
     grams = list(grams)
     inverses = [jnp.where(row == lane % CHI, 1.0, 0.0).astype(F32)] * len(grams)
     pivots = list(grams)
-    for k in range(CHI):
+    for k in range(0, CHI, 2):
         for s in range(len(grams)):
-            column = jnp.take_along_axis(grams[s], lane // CHI * CHI + k, axis=1)
-            pivot = column[k:k + 1, :]
-            pivots[s] = jnp.where(row == k, pivot, pivots[s])
-            factor = jnp.where(row > k, column * (1.0 / pivot), 0.0)
-            inverses[s] = inverses[s] - factor * inverses[s][k:k + 1, :]
-            grams[s] = grams[s] - factor * grams[s][k:k + 1, :]
+            gram, inverse = grams[s], inverses[s]
+            first = jnp.take_along_axis(gram, lane // CHI * CHI + k, axis=1)
+            second = jnp.take_along_axis(gram, lane // CHI * CHI + k + 1, axis=1)
+            over = 1.0 / first[k:k + 1]
+            first_factor = first * over
+            shared = second[k:k + 1]
+            second = second - first_factor * shared
+            step = first_factor[k + 1:k + 2]
+            gram_row, inverse_row = gram[k:k + 1], inverse[k:k + 1]
+            gram_next = gram[k + 1:k + 2] - step * gram_row
+            inverse_next = inverse[k + 1:k + 2] - step * inverse_row
+            pivots[s] = jnp.where(row == k, first[k:k + 1], jnp.where(row == k + 1, second[k + 1:k + 2], pivots[s]))
+            first_factor = jnp.where(row > k, first_factor, 0.0)
+            second_factor = jnp.where(row > k + 1, second * (1.0 / second[k + 1:k + 2]), 0.0)
+            grams[s] = gram - first_factor * gram_row - second_factor * gram_next
+            inverses[s] = inverse - first_factor * inverse_row - second_factor * inverse_next
     return [i * lax.rsqrt(p) for i, p in zip(inverses, pivots)]
 
 
@@ -75,42 +85,42 @@
     return jnp.where((row // CHI == col % CHI) & (row % CHI == col // CHI), 1.0, 0.0).astype(F32)
 
 
-def contract(g, north_east, north_west, south_east, south_west, sums, store):
-    flip_wide = flip_mask()
-    flip_matrix = flip_wide.astype(BF16)
-    at_row, at_col = iota((8, 128), 0), iota((8, 128), 1)
+def pair_sides(left, right):
+    left = jnp.dot(flip_mask().astype(BF16), left, preferred_element_type=F32).astype(BF16)
+    return left, right, left.T, right.T
+
+
+def low_pair(sides, q):
     chunk = iota((WIDE, HALF), 1) // CHI
-    turned = jnp.dot(jnp.concatenate(south_east, axis=0), flip_matrix, preferred_element_type=F32).astype(BF16)
-    turned = [turned[q * CHI:(q + 1) * CHI] for q in range(4)]
-    left_side = spread(north_east + turned)
-    left_side = jnp.dot(flip_matrix, left_side, preferred_element_type=F32).astype(BF16)
-    right_side = spread(north_west + south_west)
-    left_turned, right_turned = left_side.T, right_side.T
-    zero = jnp.zeros((), BF16)
-
-    def paired(p):
-        low = jnp.dot(jnp.where(chunk == p, right_side, zero), left_turned, preferred_element_type=F32)
-        high = jnp.dot(jnp.where(chunk == p + 4, left_side, zero), right_turned, preferred_element_type=F32)
-        return regroup(low.astype(BF16)), regroup(high.astype(BF16))
-
-    def finish(p, pairs, sums):
-        squares, traces = sums
-        raw = jnp.dot(pairs[0], pairs[1], preferred_element_type=F32)
-        square = jnp.sum(jnp.sum(raw * raw, axis=0, keepdims=True), axis=1, keepdims=True) + 1e-6
-        traced = jnp.sum(jnp.sum(raw * flip_wide, axis=0, keepdims=True), axis=1, keepdims=True)
-        store(p, (raw * (WIDE * lax.rsqrt(square))).astype(BF16))
-        here = (at_row == g) & (at_col == p)
-        return jnp.where(here, square, squares), jnp.where(here, traced, traces)
-
-    ahead = paired(0)
-    for p in range(4):
-        pairs, ahead = ahead, paired(p + 1) if p < 3 else None
-        sums = finish(p, pairs, sums)
-    return sums
+    masked = jnp.where(chunk == q, sides[1], jnp.zeros((), BF16))
+    return regroup(jnp.dot(masked, sides[2], preferred_element_type=F32).astype(BF16))
+
+
+def high_pair(sides, q):
+    chunk = iota((WIDE, HALF), 1) // CHI
+    masked = jnp.where(chunk == q, sides[0], jnp.zeros((), BF16))
+    return regroup(jnp.dot(masked, sides[3], preferred_element_type=F32).astype(BF16))
+
+
+def high_sides(south_east, south_west):
+    turned = jnp.dot(
+        jnp.concatenate(south_east, axis=0), flip_mask().astype(BF16), preferred_element_type=F32).astype(BF16)
+    both = spread([turned[q * CHI:(q + 1) * CHI] for q in range(4)] + south_west)
+    return pair_sides(both, pltpu.roll(both, HALF // 2, 1))
+
+
+def finish(g, p, low, high, sums, store):
+    squares, traces = sums
+    raw = jnp.dot(low, high, preferred_element_type=F32)
+    square = jnp.sum(jnp.sum(raw * raw, axis=0, keepdims=True), axis=1, keepdims=True) + 1e-6
+    traced = jnp.sum(jnp.sum(raw * flip_mask(), axis=0, keepdims=True), axis=1, keepdims=True)
+    store(p, (raw * (WIDE * lax.rsqrt(square))).astype(BF16))
+    here = (iota((8, 128), 0) == g) & (iota((8, 128), 1) == p)
+    return jnp.where(here, square, squares), jnp.where(here, traced, traces)
 
 
 def split_kernel(
-    nx, ny, tensors_ref, tests_ref, coarse_ref, sums_ref, ne_ref, nw_ref, halo_ref,
+    nx, ny, tensors_ref, tests_ref, coarse_ref, sums_ref, lows_ref, last_ref, halo_ref,
     held, basis_ref, low_ref, up_ref, halo_basis, halo_second, tests, in_sem, send_sem, recv_sem,
 ):
     mx, my = lax.axis_index("gx"), lax.axis_index("gy")
@@ -172,30 +182,35 @@
         coarse_ref[p] = value
 
     sums = (jnp.ones((8, 128), F32), jnp.zeros((8, 128), F32))
-    sums = contract(
-        0,
-        [basis_ref[4 * p] for p in range(4)],
-        [basis_ref[4 * p + 2] for p in range(4)],
-        [up_ref[2 * p] for p in range(4)],
-        [up_ref[2 * p + 1] for p in range(4)],
-        sums,
-        store,
-    )
+    north_east = [basis_ref[4 * p] for p in range(4)] + [basis_ref[4 * p + 3] for p in range(4)]
+    north_west = [basis_ref[4 * p + 2] for p in range(4)] + [basis_ref[4 * p + 5] for p in range(3)]
+    low_sides = pair_sides(spread(north_east), spread(north_west + north_west[:1]))
+    sides = high_sides([up_ref[2 * p] for p in range(4)], [up_ref[2 * p + 1] for p in range(4)])
+    ahead = low_pair(low_sides, 0), high_pair(sides, 0)
+    for p in range(4):
+        (low, high), ahead = ahead, (low_pair(low_sides, p + 1), high_pair(sides, p + 1)) if p < 3 else None
+        sums = finish(0, p, low, high, sums, store)
+    for p in range(3):
+        lows_ref[p] = low_pair(low_sides, p + 4)
     sums_ref[0] = sums[0]
     sums_ref[1] = sums[1]
-    for p in range(4):
-        ne_ref[p] = basis_ref[4 * p + 3]
-        if p < 3:
-            nw_ref[p] = basis_ref[4 * p + 5]
+    last_ref[0] = basis_ref[15]
     for copy in copies:
         copy.wait()
-    nw_ref[3] = halo_basis[0]
+    last_ref[1] = halo_basis[0]
     halo_ref[...] = halo_second[...]
 
 
-def join_kernel(first_ref, sums_ref, ne_ref, nw_ref, halo_ref, coarse_ref, log_ref, trace_ref, stage, out_sem):
+def join_kernel(
+    first_ref, sums_ref, lows_ref, last_ref, halo_ref, coarse_ref, log_ref, trace_ref,
+    stage, log_stage, trace_stage, out_sem,
+):
     early = [pltpu.make_async_copy(first_ref.at[p], coarse_ref.at[p, 0], out_sem.at[p]) for p in range(4)]
     late = [pltpu.make_async_copy(stage.at[p], coarse_ref.at[p, 1], out_sem.at[4 + p]) for p in range(4)]
+    small = [
+        pltpu.make_async_copy(log_stage, log_ref, out_sem.at[8]),
+        pltpu.make_async_copy(trace_stage, trace_ref, out_sem.at[9]),
+    ]
     for copy in early:
         copy.start()
 
@@ -203,19 +218,23 @@
         stage[p] = value
         late[p].start()
 
-    squares, traces = contract(
-        1,
-        [ne_ref[p] for p in range(4)],
-        [nw_ref[p] for p in range(4)],
-        [halo_ref[2 * p] for p in range(4)],
-        [halo_ref[2 * p + 1] for p in range(4)],
-        (sums_ref[0], sums_ref[1]),
-        store,
-    )
+    sides = high_sides([halo_ref[2 * p] for p in range(4)], [halo_ref[2 * p + 1] for p in range(4)])
+    edge = spread([last_ref[0], last_ref[1]] + [last_ref[0]] * 6)
+    last_sides = pair_sides(edge, pltpu.roll(edge, HALF - CHI, 1))
+    sums = (sums_ref[0], sums_ref[1])
+    ahead = lows_ref[0], high_pair(sides, 0)
+    for p in range(4):
+        low, high = ahead
+        if p < 3:
+            ahead = lows_ref[p + 1] if p < 2 else low_pair(last_sides, 0), high_pair(sides, p + 1)
+        sums = finish(1, p, low, high, sums, store)
+    squares, traces = sums
     norm = jnp.sqrt(squares)
-    log_ref[...] = jnp.log(norm)[:2, :4]
-    trace_ref[...] = (CHI * traces / norm)[:2, :4]
-    for copy in early + late:
+    log_stage[...] = jnp.log(norm)[:2, :4]
+    trace_stage[...] = (CHI * traces / norm)[:2, :4]
+    for copy in small:
+        copy.start()
+    for copy in early + late + small:
         copy.wait()
 
 
@@ -232,8 +251,8 @@
             out_shape=(
                 pltpu.VMEM((4, WIDE, WIDE), BF16),
                 pltpu.VMEM((2, 8, 128), F32),
-                pltpu.VMEM((4, CHI, WIDE), BF16),
-                pltpu.VMEM((4, CHI, WIDE), BF16),
+                pltpu.VMEM((3, WIDE, WIDE), BF16),
+                pltpu.VMEM((2, CHI, WIDE), BF16),
                 pltpu.VMEM((8, CHI, WIDE), BF16),
             ),
             in_specs=[hbm, hbm],
@@ -260,14 +279,16 @@
             join_kernel,
             out_shape=(
                 pltpu.HBM((4, 2, WIDE, WIDE), BF16),
-                jax.ShapeDtypeStruct((2, 4), F32),
-                jax.ShapeDtypeStruct((2, 4), F32),
+                pltpu.HBM((2, 4), F32),
+                pltpu.HBM((2, 4), F32),
             ),
             in_specs=[vmem] * 5,
-            out_specs=(hbm, vmem, vmem),
+            out_specs=(hbm, hbm, hbm),
             scratch_shapes=[
                 pltpu.VMEM((4, WIDE, WIDE), BF16),
-                pltpu.SemaphoreType.DMA((8,)),
+                pltpu.VMEM((2, 4), F32),
+                pltpu.VMEM((2, 4), F32),
+                pltpu.SemaphoreType.DMA((10,)),
             ],
             compiler_params=pltpu.CompilerParams(vmem_limit_bytes=24 * 2**20),
             cost_estimate=pl.CostEstimate(

time: 14.4 us -> 13.8 us (0.958)
  Pallas kernels: 13.6 us -> 13 us
    pallas_call x1, Pallas kernels: 3.48 us -> 2.89 us  [body(): pl.pallas_call(join_kernel, out_shape=(pltpu.HBM((4, 2, WIDE, WIDE), BF16...]
where the time goes in v4:
time: 13.8 us; the launch traced here: 13.6 us
  Pallas kernels  13 us (94%)
  between operations  0.64 us (5%)
    pallas_call x1, Pallas kernels, body(): pl.pallas_call(lambda *refs: split_kernel(nx, ny, *refs), out_shape=(pltp...  10.1 us
    pallas_call x1, Pallas kernels, body(): pl.pallas_call(join_kernel, out_shape=(pltpu.HBM((4, 2, WIDE, WIDE), BF16...  2.89 us

profile of v4, /device:TPU:0, one launch (start us, length us, event | category | flops | bytes accessed | tf_op | source)
XLA Modules:
  0.0 13.6 jit_solution(5832443695066526189)
XLA Ops:
  0.6 10.1 %shard_map.49 = (bf16[4,256,256]{2,1,0:T(8,128)(2,1)S(1)}, f32[2,8,128]{2,1,0:T(8,128)S(1)}, bf16[3,256,256]{2,1,0:T(8,128)(2,1)S(1)}, bf16[2,16,256]{2,1,0:T(8,128)(2,1)S(1)}, bf16[8,16,256]{2,1,0:T(8,128)(2,1)S(1)}) custom-call(bf16[8,2,256,256]{3,2,1,0:T(8,128)(2,1)} %refs_0_.1, bf16[8,2,16,256]{3,2,1,0:T(8,128)(2,1)} %refs_1_.1), custom_call_target="tpu_custom_call" | custom-call | flops 700000000 | bytes 3000000 | tf_op jit(solution)/shard_map/pallas_call | solution.py:249
  10.7 2.9 %shard_map.50 = (bf16[4,2,256,256]{3,2,1,0:T(8,128)(2,1)}, f32[2,4]{1,0:T(2,128)}, f32[2,4]{1,0:T(2,128)}) custom-call(bf16[4,256,256]{2,1,0:T(8,128)(2,1)S(1)} %get-tuple-element.11.first_ref, f32[2,8,128]{2,1,0:T(8,128)S(1)} %get-tuple-element.12.sums_ref, bf16[3,256,256]{2,1,0:T(8,128)(2,1)S(1)} %get-tuple-element.13.lows_ref, ...), custom_call_target="tpu_custom_call" | custom-call | flops 300000000 | bytes 1000000 | tf_op jit(solution)/shard_map/pallas_call | solution.py:278

commit v5 on v4

--- a/solution.py
+++ b/solution.py
@@ -28,6 +28,10 @@
             if i & step:
                 continue
             first, other = rows[i], rows[i + step]
+            if step == 4:
+                moved = pltpu.roll(jnp.where(low, other, first), HALF // 2, 1)
+                rows[i], rows[i + step] = jnp.where(low, first, moved), jnp.where(low, moved, other)
+                continue
             rows[i] = jnp.where(low, first, pltpu.roll(other, CHI * step, 1))
             rows[i + step] = jnp.where(low, pltpu.roll(first, HALF - CHI * step, 1), other)
     return rows
@@ -157,7 +161,6 @@
         basis = lax.dot_general(block, part, NN, precision=lax.Precision.HIGHEST, preferred_element_type=F32)
         basis_ref[pl.ds(8 * side, 8)] = basis.astype(BF16).reshape(8, CHI, WIDE)
 
-    pl.semaphore_wait(barrier, 3)
     copies = [
         pltpu.make_async_remote_copy(
             basis_ref.at[1], halo_basis.at[0], send_sem.at[0], recv_sem.at[0],
@@ -169,12 +172,14 @@
             low_ref.at[pl.ds(1, 7)], halo_second.at[pl.ds(0, 7)], send_sem.at[2], recv_sem.at[2],
             device_id=(mx, below), device_id_type=MESH),
     ]
-    copies[0].start()
+    def send():
+        pl.semaphore_wait(barrier, 3)
+        for copy in copies:
+            copy.start()
+
     for x in range(8):
         low_ref[x] = jnp.dot(basis_ref[2 * x], held[x, 0], preferred_element_type=F32).astype(BF16)
-        if x == 0:
-            copies[1].start()
-    copies[2].start()
+    pl.when(my != 0)(send)
     for x in range(8):
         up_ref[x] = jnp.dot(basis_ref[2 * x + 1], held[x, 1], preferred_element_type=F32).astype(BF16)
 
@@ -195,6 +200,7 @@
     sums_ref[0] = sums[0]
     sums_ref[1] = sums[1]
     last_ref[0] = basis_ref[15]
+    pl.when(my == 0)(send)
     for copy in copies:
         copy.wait()
     last_ref[1] = halo_basis[0]

time: 13.8 us -> 14.8 us (1.072)
  the two profiles are of different devices: /device:TPU:0 before, /device:TPU:1 now
where the time goes in v5:
time: 14.8 us; the launch traced here: 14.6 us
  Pallas kernels  14 us (95%)
  between operations  0.64 us (4%)
    pallas_call x1, Pallas kernels, body(): pl.pallas_call(lambda *refs: split_kernel(nx, ny, *refs), out_shape=(pltp...  11.1 us
    pallas_call x1, Pallas kernels, body(): pl.pallas_call(join_kernel, out_shape=(pltpu.HBM((4, 2, WIDE, WIDE), BF16...  2.86 us

profile of v5, /device:TPU:1, one launch (start us, length us, event | category | flops | bytes accessed | tf_op | source)
XLA Modules:
  0.0 14.6 jit_solution(7031853886814630705)
XLA Ops:
  0.6 11.1 %shard_map.49 = (bf16[4,256,256]{2,1,0:T(8,128)(2,1)S(1)}, f32[2,8,128]{2,1,0:T(8,128)S(1)}, bf16[3,256,256]{2,1,0:T(8,128)(2,1)S(1)}, bf16[2,16,256]{2,1,0:T(8,128)(2,1)S(1)}, bf16[8,16,256]{2,1,0:T(8,128)(2,1)S(1)}) custom-call(bf16[8,2,256,256]{3,2,1,0:T(8,128)(2,1)} %refs_0_.1, bf16[8,2,16,256]{3,2,1,0:T(8,128)(2,1)} %refs_1_.1), custom_call_target="tpu_custom_call" | custom-call | flops 700000000 | bytes 3000000 | tf_op jit(solution)/shard_map/pallas_call | solution.py:255
  11.8 2.9 %shard_map.50 = (bf16[4,2,256,256]{3,2,1,0:T(8,128)(2,1)}, f32[2,4]{1,0:T(2,128)}, f32[2,4]{1,0:T(2,128)}) custom-call(bf16[4,256,256]{2,1,0:T(8,128)(2,1)S(1)} %get-tuple-element.11.first_ref, f32[2,8,128]{2,1,0:T(8,128)S(1)} %get-tuple-element.12.sums_ref, bf16[3,256,256]{2,1,0:T(8,128)(2,1)S(1)} %get-tuple-element.13.lows_ref, ...), custom_call_target="tpu_custom_call" | custom-call | flops 300000000 | bytes 1000000 | tf_op jit(solution)/shard_map/pallas_call | solution.py:284

commit v6 on v5

--- a/solution.py
+++ b/solution.py
@@ -139,26 +139,29 @@
     for target in ((right, my), (mx, above), (right, above)):
         pl.semaphore_signal(barrier, inc=1, device_id=target, device_id_type=MESH)
 
-    sketches = []
     loads[8].wait()
-    for x in range(8):
-        loads[x].wait()
-        for y in range(2):
-            sketches.append(lax.dot_general(tests[x, y], held[x, y], NT, preferred_element_type=F32))
-    sketch = jnp.concatenate(sketches, axis=0)
     chunk = iota((CHI, HALF), 1) // CHI
-    grams = []
+    tall = iota((WIDE, HALF), 1) // CHI
+    parts, grams = [], []
     for side in range(2):
-        part = sketch[side * HALF:(side + 1) * HALF]
-        product = lax.dot_general(part, part, NT, precision=lax.Precision.HIGHEST, preferred_element_type=F32)
-        gram = jnp.zeros((CHI, HALF), F32)
+        across = jnp.concatenate([tests[4 * side + n // 2, n % 2] for n in range(8)], axis=0).T
+        sketch = None
         for n in range(8):
-            gram = gram + jnp.where(chunk == n, product[n * CHI:(n + 1) * CHI], 0.0)
+            x, y = 4 * side + n // 2, n % 2
+            if y == 0:
+                loads[x].wait()
+            wide = jnp.dot(held[x, y], across, preferred_element_type=F32)
+            sketch = wide if n == 0 else jnp.where(tall == n, wide, sketch)
+        part = sketch.T
+        product = jnp.dot(part, sketch, precision=lax.Precision.HIGHEST, preferred_element_type=F32)
+        gram = product[:CHI]
+        for n in range(1, 8):
+            gram = jnp.where(chunk == n, product[n * CHI:(n + 1) * CHI], gram)
+        parts.append(part)
         grams.append(gram)
     for side, inverse in enumerate(eliminate(grams)):
-        part = sketch[side * HALF:(side + 1) * HALF]
         block = jnp.concatenate([jnp.where(chunk == n, inverse, 0.0) for n in range(8)], axis=0)
-        basis = lax.dot_general(block, part, NN, precision=lax.Precision.HIGHEST, preferred_element_type=F32)
+        basis = jnp.dot(block, parts[side], precision=lax.Precision.HIGHEST, preferred_element_type=F32)
         basis_ref[pl.ds(8 * side, 8)] = basis.astype(BF16).reshape(8, CHI, WIDE)
 
     copies = [
@@ -179,7 +182,8 @@
 
     for x in range(8):
         low_ref[x] = jnp.dot(basis_ref[2 * x], held[x, 0], preferred_element_type=F32).astype(BF16)
-    pl.when(my != 0)(send)
+    first_chip = (my == 0) & (mx < 2)
+    pl.when(jnp.logical_not(first_chip))(send)
     for x in range(8):
         up_ref[x] = jnp.dot(basis_ref[2 * x + 1], held[x, 1], preferred_element_type=F32).astype(BF16)
 
@@ -191,16 +195,16 @@
     north_west = [basis_ref[4 * p + 2] for p in range(4)] + [basis_ref[4 * p + 5] for p in range(3)]
     low_sides = pair_sides(spread(north_east), spread(north_west + north_west[:1]))
     sides = high_sides([up_ref[2 * p] for p in range(4)], [up_ref[2 * p + 1] for p in range(4)])
+    for p in range(3):
+        lows_ref[p] = low_pair(low_sides, p + 4)
     ahead = low_pair(low_sides, 0), high_pair(sides, 0)
+    pl.when(first_chip)(send)
     for p in range(4):
         (low, high), ahead = ahead, (low_pair(low_sides, p + 1), high_pair(sides, p + 1)) if p < 3 else None
         sums = finish(0, p, low, high, sums, store)
-    for p in range(3):
-        lows_ref[p] = low_pair(low_sides, p + 4)
     sums_ref[0] = sums[0]
     sums_ref[1] = sums[1]
     last_ref[0] = basis_ref[15]
-    pl.when(my == 0)(send)
     for copy in copies:
         copy.wait()
     last_ref[1] = halo_basis[0]

time: 14.8 us -> 13.6 us (0.919)
  the two profiles are of different devices: /device:TPU:1 before, /device:TPU:0 now
where the time goes in v6:
time: 13.6 us; the launch traced here: 13.4 us
  Pallas kernels  12.8 us (94%)
  between operations  0.64 us (5%)
    pallas_call x1, Pallas kernels, body(): pl.pallas_call(lambda *refs: split_kernel(nx, ny, *refs), out_shape=(pltp...  9.95 us
    pallas_call x1, Pallas kernels, body(): pl.pallas_call(join_kernel, out_shape=(pltpu.HBM((4, 2, WIDE, WIDE), BF16...  2.86 us

profile of v6, /device:TPU:0, one launch (start us, length us, event | category | flops | bytes accessed | tf_op | source)
XLA Modules:
  0.0 13.4 jit_solution(5457700260055361883)
XLA Ops:
  0.6 9.9 %shard_map.49 = (bf16[4,256,256]{2,1,0:T(8,128)(2,1)S(1)}, f32[2,8,128]{2,1,0:T(8,128)S(1)}, bf16[3,256,256]{2,1,0:T(8,128)(2,1)S(1)}, bf16[2,16,256]{2,1,0:T(8,128)(2,1)S(1)}, bf16[8,16,256]{2,1,0:T(8,128)(2,1)S(1)}) custom-call(bf16[8,2,256,256]{3,2,1,0:T(8,128)(2,1)} %refs_0_.1, bf16[8,2,16,256]{3,2,1,0:T(8,128)(2,1)} %refs_1_.1), custom_call_target="tpu_custom_call" | custom-call | flops 700000000 | bytes 3000000 | tf_op jit(solution)/shard_map/pallas_call | solution.py:259
  10.6 2.9 %shard_map.50 = (bf16[4,2,256,256]{3,2,1,0:T(8,128)(2,1)}, f32[2,4]{1,0:T(2,128)}, f32[2,4]{1,0:T(2,128)}) custom-call(bf16[4,256,256]{2,1,0:T(8,128)(2,1)S(1)} %get-tuple-element.11.first_ref, f32[2,8,128]{2,1,0:T(8,128)S(1)} %get-tuple-element.12.sums_ref, bf16[3,256,256]{2,1,0:T(8,128)(2,1)S(1)} %get-tuple-element.13.lows_ref, ...), custom_call_target="tpu_custom_call" | custom-call | flops 300000000 | bytes 1000000 | tf_op jit(solution)/shard_map/pallas_call | solution.py:288

commit v7 on v6

--- a/solution.py
+++ b/solution.py
@@ -125,12 +125,16 @@
 
 def split_kernel(
     nx, ny, tensors_ref, tests_ref, coarse_ref, sums_ref, lows_ref, last_ref, halo_ref,
-    held, basis_ref, low_ref, up_ref, halo_basis, halo_second, tests, in_sem, send_sem, recv_sem,
+    held, basis_ref, low_ref, up_ref, halo_basis, halo_second, tests, own_lows, in_sem, send_sem, recv_sem,
 ):
     mx, my = lax.axis_index("gx"), lax.axis_index("gy")
     right, left = lax.rem(mx + 1, nx), lax.rem(mx + nx - 1, nx)
     above, below = lax.rem(my + 1, ny), lax.rem(my + ny - 1, ny)
-    loads = [pltpu.make_async_copy(tensors_ref.at[c], held.at[c], in_sem.at[c]) for c in range(8)]
+    loads = [
+        pltpu.make_async_copy(
+            tensors_ref.at[pl.ds(2 * c, 2), y], held.at[y, pl.ds(2 * c, 2)], in_sem.at[4 * y + c])
+        for y in range(2) for c in range(4)
+    ]
     loads.append(pltpu.make_async_copy(tests_ref, tests, in_sem.at[8]))
     loads[8].start()
     for load in loads[:8]:
@@ -141,32 +145,29 @@
 
     loads[8].wait()
     chunk = iota((CHI, HALF), 1) // CHI
-    tall = iota((WIDE, HALF), 1) // CHI
-    parts, grams = [], []
-    for side in range(2):
-        across = jnp.concatenate([tests[4 * side + n // 2, n % 2] for n in range(8)], axis=0).T
-        sketch = None
-        for n in range(8):
-            x, y = 4 * side + n // 2, n % 2
-            if y == 0:
-                loads[x].wait()
-            wide = jnp.dot(held[x, y], across, preferred_element_type=F32)
-            sketch = wide if n == 0 else jnp.where(tall == n, wide, sketch)
-        part = sketch.T
-        product = jnp.dot(part, sketch, precision=lax.Precision.HIGHEST, preferred_element_type=F32)
+
+    def sketch_row(y):
+        sketches = []
+        for x in range(8):
+            if x % 2 == 0:
+                loads[4 * y + x // 2].wait()
+            sketches.append(lax.dot_general(tests[x, y], held[y, x], NT, preferred_element_type=F32))
+        part = jnp.concatenate(sketches, axis=0)
+        product = lax.dot_general(part, part, NT, precision=lax.Precision.HIGHEST, preferred_element_type=F32)
         gram = product[:CHI]
         for n in range(1, 8):
             gram = jnp.where(chunk == n, product[n * CHI:(n + 1) * CHI], gram)
-        parts.append(part)
-        grams.append(gram)
-    for side, inverse in enumerate(eliminate(grams)):
+        return part, gram
+
+    def basis_row(y, part, gram):
+        inverse = eliminate([gram])[0]
         block = jnp.concatenate([jnp.where(chunk == n, inverse, 0.0) for n in range(8)], axis=0)
-        basis = jnp.dot(block, parts[side], precision=lax.Precision.HIGHEST, preferred_element_type=F32)
-        basis_ref[pl.ds(8 * side, 8)] = basis.astype(BF16).reshape(8, CHI, WIDE)
+        basis = jnp.dot(block, part, precision=lax.Precision.HIGHEST, preferred_element_type=F32)
+        basis_ref[y] = basis.astype(BF16).reshape(8, CHI, WIDE)
 
     copies = [
         pltpu.make_async_remote_copy(
-            basis_ref.at[1], halo_basis.at[0], send_sem.at[0], recv_sem.at[0],
+            basis_ref.at[1, 0], halo_basis.at[0], send_sem.at[0], recv_sem.at[0],
             device_id=(left, my), device_id_type=MESH),
         pltpu.make_async_remote_copy(
             low_ref.at[0], halo_second.at[7], send_sem.at[1], recv_sem.at[1],
@@ -175,36 +176,44 @@
             low_ref.at[pl.ds(1, 7)], halo_second.at[pl.ds(0, 7)], send_sem.at[2], recv_sem.at[2],
             device_id=(mx, below), device_id_type=MESH),
     ]
-    def send():
+    def send_seconds():
         pl.semaphore_wait(barrier, 3)
-        for copy in copies:
-            copy.start()
-
+        copies[1].start()
+        copies[2].start()
+
+    lower = sketch_row(0)
+    upper = sketch_row(1)
+    basis_row(0, *lower)
     for x in range(8):
-        low_ref[x] = jnp.dot(basis_ref[2 * x], held[x, 0], preferred_element_type=F32).astype(BF16)
+        low_ref[x] = jnp.dot(basis_ref[0, x], held[0, x], preferred_element_type=F32).astype(BF16)
     first_chip = (my == 0) & (mx < 2)
-    pl.when(jnp.logical_not(first_chip))(send)
+    pl.when(jnp.logical_not(first_chip))(send_seconds)
+    basis_row(1, *upper)
+    both = spread([basis_ref[0, 2 * p] for p in range(4)] + [basis_ref[0, 2 * p + 1] for p in range(4)])
+    low_sides = pair_sides(both, pltpu.roll(both, HALF // 2, 1))
+    for p in range(4):
+        own_lows[p] = low_pair(low_sides, p)
+    pl.when(first_chip)(send_seconds)
+    copies[0].start()
     for x in range(8):
-        up_ref[x] = jnp.dot(basis_ref[2 * x + 1], held[x, 1], preferred_element_type=F32).astype(BF16)
+        up_ref[x] = jnp.dot(basis_ref[1, x], held[1, x], preferred_element_type=F32).astype(BF16)
 
     def store(p, value):
         coarse_ref[p] = value
 
     sums = (jnp.ones((8, 128), F32), jnp.zeros((8, 128), F32))
-    north_east = [basis_ref[4 * p] for p in range(4)] + [basis_ref[4 * p + 3] for p in range(4)]
-    north_west = [basis_ref[4 * p + 2] for p in range(4)] + [basis_ref[4 * p + 5] for p in range(3)]
-    low_sides = pair_sides(spread(north_east), spread(north_west + north_west[:1]))
     sides = high_sides([up_ref[2 * p] for p in range(4)], [up_ref[2 * p + 1] for p in range(4)])
-    for p in range(3):
-        lows_ref[p] = low_pair(low_sides, p + 4)
-    ahead = low_pair(low_sides, 0), high_pair(sides, 0)
-    pl.when(first_chip)(send)
+    both = spread([basis_ref[1, 2 * p + 1] for p in range(4)] + [basis_ref[1, (2 * p + 2) % 8] for p in range(4)])
+    low_sides = pair_sides(both, pltpu.roll(both, HALF // 2, 1))
+    ahead = high_pair(sides, 0)
     for p in range(4):
-        (low, high), ahead = ahead, (low_pair(low_sides, p + 1), high_pair(sides, p + 1)) if p < 3 else None
-        sums = finish(0, p, low, high, sums, store)
+        high, ahead = ahead, high_pair(sides, p + 1) if p < 3 else None
+        sums = finish(0, p, own_lows[p], high, sums, store)
+        if p < 3:
+            lows_ref[p] = low_pair(low_sides, p)
     sums_ref[0] = sums[0]
     sums_ref[1] = sums[1]
-    last_ref[0] = basis_ref[15]
+    last_ref[0] = basis_ref[1, 7]
     for copy in copies:
         copy.wait()
     last_ref[1] = halo_basis[0]
@@ -268,13 +277,14 @@
             in_specs=[hbm, hbm],
             out_specs=(vmem,) * 5,
             scratch_shapes=[
-                pltpu.VMEM((8, 2, WIDE, WIDE), BF16),
-                pltpu.VMEM((16, CHI, WIDE), BF16),
+                pltpu.VMEM((2, 8, WIDE, WIDE), BF16),
+                pltpu.VMEM((2, 8, CHI, WIDE), BF16),
                 pltpu.VMEM((8, CHI, WIDE), BF16),
                 pltpu.VMEM((8, CHI, WIDE), BF16),
                 pltpu.VMEM((1, CHI, WIDE), BF16),
                 pltpu.VMEM((8, CHI, WIDE), BF16),
                 pltpu.VMEM((8, 2, CHI, WIDE), BF16),
+                pltpu.VMEM((4, WIDE, WIDE), BF16),
                 pltpu.SemaphoreType.DMA((9,)),
                 pltpu.SemaphoreType.DMA((3,)),
                 pltpu.SemaphoreType.DMA((3,)),

time: 13.6 us -> 13.9 us (1.022)
  the two profiles are of different devices: /device:TPU:0 before, /device:TPU:1 now
where the time goes in v7:
time: 13.9 us; the launch traced here: 13.8 us
  Pallas kernels  13.1 us (94%)
  between operations  0.64 us (5%)
    pallas_call x1, Pallas kernels, body(): pl.pallas_call(lambda *refs: split_kernel(nx, ny, *refs), out_shape=(pltp...  10.3 us
    pallas_call x1, Pallas kernels, body(): pl.pallas_call(join_kernel, out_shape=(pltpu.HBM((4, 2, WIDE, WIDE), BF16...  2.86 us

profile of v7, /device:TPU:1, one launch (start us, length us, event | category | flops | bytes accessed | tf_op | source)
XLA Modules:
  0.0 13.8 jit_solution(5538473760637781274)
XLA Ops:
  0.6 10.3 %shard_map.49 = (bf16[4,256,256]{2,1,0:T(8,128)(2,1)S(1)}, f32[2,8,128]{2,1,0:T(8,128)S(1)}, bf16[3,256,256]{2,1,0:T(8,128)(2,1)S(1)}, bf16[2,16,256]{2,1,0:T(8,128)(2,1)S(1)}, bf16[8,16,256]{2,1,0:T(8,128)(2,1)S(1)}) custom-call(bf16[8,2,256,256]{3,2,1,0:T(8,128)(2,1)} %refs_0_.1, bf16[8,2,16,256]{3,2,1,0:T(8,128)(2,1)} %refs_1_.1), custom_call_target="tpu_custom_call" | custom-call | flops 700000000 | bytes 3000000 | tf_op jit(solution)/shard_map/pallas_call | solution.py:268
  10.9 2.9 %shard_map.50 = (bf16[4,2,256,256]{3,2,1,0:T(8,128)(2,1)}, f32[2,4]{1,0:T(2,128)}, f32[2,4]{1,0:T(2,128)}) custom-call(bf16[4,256,256]{2,1,0:T(8,128)(2,1)S(1)} %get-tuple-element.11.first_ref, f32[2,8,128]{2,1,0:T(8,128)S(1)} %get-tuple-element.12.sums_ref, bf16[3,256,256]{2,1,0:T(8,128)(2,1)S(1)} %get-tuple-element.13.lows_ref, ...), custom_call_target="tpu_custom_call" | custom-call | flops 300000000 | bytes 1000000 | tf_op jit(solution)/shard_map/pallas_call | solution.py:298

commit v8 on v6

--- a/solution.py
+++ b/solution.py
@@ -60,27 +60,20 @@
 def eliminate(grams):
     row = iota(grams[0].shape, 0)
     lane = iota(grams[0].shape, 1)
-    grams = list(grams)
+    ids = range(len(grams))
+    columns = [[jnp.take_along_axis(g, lane // CHI * CHI + k, axis=1) for k in range(CHI)] for g in grams]
     inverses = [jnp.where(row == lane % CHI, 1.0, 0.0).astype(F32)] * len(grams)
     pivots = list(grams)
-    for k in range(0, CHI, 2):
-        for s in range(len(grams)):
-            gram, inverse = grams[s], inverses[s]
-            first = jnp.take_along_axis(gram, lane // CHI * CHI + k, axis=1)
-            second = jnp.take_along_axis(gram, lane // CHI * CHI + k + 1, axis=1)
-            over = 1.0 / first[k:k + 1]
-            first_factor = first * over
-            shared = second[k:k + 1]
-            second = second - first_factor * shared
-            step = first_factor[k + 1:k + 2]
-            gram_row, inverse_row = gram[k:k + 1], inverse[k:k + 1]
-            gram_next = gram[k + 1:k + 2] - step * gram_row
-            inverse_next = inverse[k + 1:k + 2] - step * inverse_row
-            pivots[s] = jnp.where(row == k, first[k:k + 1], jnp.where(row == k + 1, second[k + 1:k + 2], pivots[s]))
-            first_factor = jnp.where(row > k, first_factor, 0.0)
-            second_factor = jnp.where(row > k + 1, second * (1.0 / second[k + 1:k + 2]), 0.0)
-            grams[s] = gram - first_factor * gram_row - second_factor * gram_next
-            inverses[s] = inverse - first_factor * inverse_row - second_factor * inverse_next
+    for k in range(CHI):
+        pivot = [columns[s][k][k:k + 1] for s in ids]
+        factor = [columns[s][k] * (1.0 / pivot[s]) for s in ids]
+        for later in range(k + 1, CHI):
+            for s in ids:
+                columns[s][later] = columns[s][later] - factor[s] * columns[s][later][k:k + 1]
+        for s in ids:
+            pivots[s] = jnp.where(row == k, pivot[s], pivots[s])
+            below = jnp.where(row > k, factor[s], 0.0)
+            inverses[s] = inverses[s] - below * inverses[s][k:k + 1]
     return [i * lax.rsqrt(p) for i, p in zip(inverses, pivots)]
 
 
@@ -141,19 +134,16 @@
 
     loads[8].wait()
     chunk = iota((CHI, HALF), 1) // CHI
-    tall = iota((WIDE, HALF), 1) // CHI
     parts, grams = [], []
     for side in range(2):
-        across = jnp.concatenate([tests[4 * side + n // 2, n % 2] for n in range(8)], axis=0).T
-        sketch = None
+        sketches = []
         for n in range(8):
             x, y = 4 * side + n // 2, n % 2
             if y == 0:
                 loads[x].wait()
-            wide = jnp.dot(held[x, y], across, preferred_element_type=F32)
-            sketch = wide if n == 0 else jnp.where(tall == n, wide, sketch)
-        part = sketch.T
-        product = jnp.dot(part, sketch, precision=lax.Precision.HIGHEST, preferred_element_type=F32)
+            sketches.append(lax.dot_general(tests[x, y], held[x, y], NT, preferred_element_type=F32))
+        part = jnp.concatenate(sketches, axis=0)
+        product = lax.dot_general(part, part, NT, precision=lax.Precision.HIGHEST, preferred_element_type=F32)
         gram = product[:CHI]
         for n in range(1, 8):
             gram = jnp.where(chunk == n, product[n * CHI:(n + 1) * CHI], gram)

time: 13.6 us -> 12.9 us (0.949)
  Pallas kernels: 12.8 us -> 12.1 us
    pallas_call x1, Pallas kernels: 9.95 us -> 9.24 us  [body(): pl.pallas_call(lambda *refs: split_kernel(nx, ny, *refs), out_shape=(pltp...]
where the time goes in v8:
time: 12.9 us; the launch traced here: 12.7 us
  Pallas kernels  12.1 us (94%)
  between operations  0.64 us (5%)
    pallas_call x1, Pallas kernels, body(): pl.pallas_call(lambda *refs: split_kernel(nx, ny, *refs), out_shape=(pltp...  9.24 us
    pallas_call x1, Pallas kernels, body(): pl.pallas_call(join_kernel, out_shape=(pltpu.HBM((4, 2, WIDE, WIDE), BF16...  2.86 us

profile of v8, /device:TPU:0, one launch (start us, length us, event | category | flops | bytes accessed | tf_op | source)
XLA Modules:
  0.0 12.7 jit_solution(3120859404422129258)
XLA Ops:
  0.6 9.2 %shard_map.49 = (bf16[4,256,256]{2,1,0:T(8,128)(2,1)S(1)}, f32[2,8,128]{2,1,0:T(8,128)S(1)}, bf16[3,256,256]{2,1,0:T(8,128)(2,1)S(1)}, bf16[2,16,256]{2,1,0:T(8,128)(2,1)S(1)}, bf16[8,16,256]{2,1,0:T(8,128)(2,1)S(1)}) custom-call(bf16[8,2,256,256]{3,2,1,0:T(8,128)(2,1)} %refs_0_.1, bf16[8,2,16,256]{3,2,1,0:T(8,128)(2,1)} %refs_1_.1), custom_call_target="tpu_custom_call" | custom-call | flops 700000000 | bytes 3000000 | tf_op jit(solution)/shard_map/pallas_call | solution.py:249
  9.9 2.9 %shard_map.50 = (bf16[4,2,256,256]{3,2,1,0:T(8,128)(2,1)}, f32[2,4]{1,0:T(2,128)}, f32[2,4]{1,0:T(2,128)}) custom-call(bf16[4,256,256]{2,1,0:T(8,128)(2,1)S(1)} %get-tuple-element.11.first_ref, f32[2,8,128]{2,1,0:T(8,128)S(1)} %get-tuple-element.12.sums_ref, bf16[3,256,256]{2,1,0:T(8,128)(2,1)S(1)} %get-tuple-element.13.lows_ref, ...), custom_call_target="tpu_custom_call" | custom-call | flops 300000000 | bytes 1000000 | tf_op jit(solution)/shard_map/pallas_call | solution.py:278

commit v9 on v8

--- a/solution.py
+++ b/solution.py
@@ -77,6 +77,17 @@
     return [i * lax.rsqrt(p) for i, p in zip(inverses, pivots)]
 
 
+def halves_of(x):
+    high = x.astype(BF16)
+    return high, (x - high.astype(F32)).astype(BF16)
+
+
+def product_of(left, right, dims):
+    rows = left[0].shape[0]
+    main = lax.dot_general(jnp.concatenate(left, axis=0), right[0], dims, preferred_element_type=F32)
+    return main[:rows] + (main[rows:] + lax.dot_general(left[0], right[1], dims, preferred_element_type=F32))
+
+
 def flip_mask():
     row, col = iota((WIDE, WIDE), 0), iota((WIDE, WIDE), 1)
     return jnp.where((row // CHI == col % CHI) & (row % CHI == col // CHI), 1.0, 0.0).astype(F32)
@@ -142,8 +153,8 @@
             if y == 0:
                 loads[x].wait()
             sketches.append(lax.dot_general(tests[x, y], held[x, y], NT, preferred_element_type=F32))
-        part = jnp.concatenate(sketches, axis=0)
-        product = lax.dot_general(part, part, NT, precision=lax.Precision.HIGHEST, preferred_element_type=F32)
+        part = halves_of(jnp.concatenate(sketches, axis=0))
+        product = product_of(part, part, NT)
         gram = product[:CHI]
         for n in range(1, 8):
             gram = jnp.where(chunk == n, product[n * CHI:(n + 1) * CHI], gram)
@@ -151,7 +162,7 @@
         grams.append(gram)
     for side, inverse in enumerate(eliminate(grams)):
         block = jnp.concatenate([jnp.where(chunk == n, inverse, 0.0) for n in range(8)], axis=0)
-        basis = jnp.dot(block, parts[side], precision=lax.Precision.HIGHEST, preferred_element_type=F32)
+        basis = product_of(halves_of(block), parts[side], NN)
         basis_ref[pl.ds(8 * side, 8)] = basis.astype(BF16).reshape(8, CHI, WIDE)
 
     copies = [
@@ -162,18 +173,28 @@
             low_ref.at[0], halo_second.at[7], send_sem.at[1], recv_sem.at[1],
             device_id=(left, below), device_id_type=MESH),
         pltpu.make_async_remote_copy(
-            low_ref.at[pl.ds(1, 7)], halo_second.at[pl.ds(0, 7)], send_sem.at[2], recv_sem.at[2],
+            low_ref.at[pl.ds(1, 3)], halo_second.at[pl.ds(0, 3)], send_sem.at[2], recv_sem.at[2],
+            device_id=(mx, below), device_id_type=MESH),
+        pltpu.make_async_remote_copy(
+            low_ref.at[pl.ds(4, 4)], halo_second.at[pl.ds(3, 4)], send_sem.at[3], recv_sem.at[3],
             device_id=(mx, below), device_id_type=MESH),
     ]
-    def send():
+    def send_early():
         pl.semaphore_wait(barrier, 3)
-        for copy in copies:
+        for copy in copies[:3]:
             copy.start()
 
-    for x in range(8):
+    def send_all():
+        send_early()
+        copies[3].start()
+
+    first_chip = (my == 0) & (mx < 2)
+    for x in range(4):
         low_ref[x] = jnp.dot(basis_ref[2 * x], held[x, 0], preferred_element_type=F32).astype(BF16)
-    first_chip = (my == 0) & (mx < 2)
-    pl.when(jnp.logical_not(first_chip))(send)
+    pl.when(jnp.logical_not(first_chip))(send_early)
+    for x in range(4, 8):
+        low_ref[x] = jnp.dot(basis_ref[2 * x], held[x, 0], preferred_element_type=F32).astype(BF16)
+    pl.when(jnp.logical_not(first_chip))(copies[3].start)
     for x in range(8):
         up_ref[x] = jnp.dot(basis_ref[2 * x + 1], held[x, 1], preferred_element_type=F32).astype(BF16)
 
@@ -188,7 +209,7 @@
     for p in range(3):
         lows_ref[p] = low_pair(low_sides, p + 4)
     ahead = low_pair(low_sides, 0), high_pair(sides, 0)
-    pl.when(first_chip)(send)
+    pl.when(first_chip)(send_all)
     for p in range(4):
         (low, high), ahead = ahead, (low_pair(low_sides, p + 1), high_pair(sides, p + 1)) if p < 3 else None
         sums = finish(0, p, low, high, sums, store)
@@ -266,8 +287,8 @@
                 pltpu.VMEM((8, CHI, WIDE), BF16),
                 pltpu.VMEM((8, 2, CHI, WIDE), BF16),
                 pltpu.SemaphoreType.DMA((9,)),
-                pltpu.SemaphoreType.DMA((3,)),
-                pltpu.SemaphoreType.DMA((3,)),
+                pltpu.SemaphoreType.DMA((4,)),
+                pltpu.SemaphoreType.DMA((4,)),
             ],
             compiler_params=pltpu.CompilerParams(
                 collective_id=0, has_side_effects=True, vmem_limit_bytes=24 * 2**20),

time: 12.9 us -> 12.5 us (0.969)
  Pallas kernels: 12.1 us -> 11.7 us
    pallas_call x1, Pallas kernels: 9.24 us -> 8.83 us  [body(): pl.pallas_call(lambda *refs: split_kernel(nx, ny, *refs), out_shape=(pltp...]
where the time goes in v9:
time: 12.5 us; the launch traced here: 12.3 us
  Pallas kernels  11.7 us (94%)
  between operations  0.64 us (5%)
    pallas_call x1, Pallas kernels, body(): pl.pallas_call(lambda *refs: split_kernel(nx, ny, *refs), out_shape=(pltp...  8.83 us
    pallas_call x1, Pallas kernels, body(): pl.pallas_call(join_kernel, out_shape=(pltpu.HBM((4, 2, WIDE, WIDE), BF16...  2.85 us

profile of v9, /device:TPU:0, one launch (start us, length us, event | category | flops | bytes accessed | tf_op | source)
XLA Modules:
  0.0 12.3 jit_solution(1877234353953754360)
XLA Ops:
  0.6 8.8 %shard_map.49 = (bf16[4,256,256]{2,1,0:T(8,128)(2,1)S(1)}, f32[2,8,128]{2,1,0:T(8,128)S(1)}, bf16[3,256,256]{2,1,0:T(8,128)(2,1)S(1)}, bf16[2,16,256]{2,1,0:T(8,128)(2,1)S(1)}, bf16[8,16,256]{2,1,0:T(8,128)(2,1)S(1)}) custom-call(bf16[8,2,256,256]{3,2,1,0:T(8,128)(2,1)} %refs_0_.1, bf16[8,2,16,256]{3,2,1,0:T(8,128)(2,1)} %refs_1_.1), custom_call_target="tpu_custom_call" | custom-call | flops 700000000 | bytes 3000000 | tf_op jit(solution)/shard_map/pallas_call | solution.py:270
  9.5 2.9 %shard_map.50 = (bf16[4,2,256,256]{3,2,1,0:T(8,128)(2,1)}, f32[2,4]{1,0:T(2,128)}, f32[2,4]{1,0:T(2,128)}) custom-call(bf16[4,256,256]{2,1,0:T(8,128)(2,1)S(1)} %get-tuple-element.11.first_ref, f32[2,8,128]{2,1,0:T(8,128)S(1)} %get-tuple-element.12.sums_ref, bf16[3,256,256]{2,1,0:T(8,128)(2,1)S(1)} %get-tuple-element.13.lows_ref, ...), custom_call_target="tpu_custom_call" | custom-call | flops 300000000 | bytes 1000000 | tf_op jit(solution)/shard_map/pallas_call | solution.py:299
